TPU v7x, 32 devices: a whole 2x2x4 slice. The times are simulated.
32 devices in a mesh: seq: 8 (over z, x), head: 4 (over y, core).
Axes of the slice: x: 2, y: 2, z: 4, core: 2. Of those that a mesh axis runs over, the one named last changes fastest.
Arguments:
- tokens_in: bfloat16 [4, 2048, 768], P(None, 'seq', 'head'), may hold values from -6 to 6
- out_grad: bfloat16 [4, 2048, 768], P(None, 'seq', 'head'), may hold values from -6 to 6
- lengths: int32 [4, 4], replicated, may hold values from 1 to 1920, as said below
- norm_gain: bfloat16 [768], P('head'), may hold values from 0.5 to 1.5
- proj_z: bfloat16 [768, 1536], P(None, 'head'), may hold values from -0.21875 to 0.21875
- proj_x: bfloat16 [768, 1536], P(None, 'head'), may hold values from -0.21875 to 0.21875
- proj_bc: bfloat16 [768, 256], P(None, 'head'), may hold values from -0.21875 to 0.21875
- proj_dt: bfloat16 [768, 24], P(None, 'head'), may hold values from -0.21875 to 0.21875
- conv_x: bfloat16 [4, 1536], P(None, 'head'), may hold values from -3 to 3
- conv_bc: bfloat16 [4, 256], P(None, 'head'), may hold values from -3 to 3
- bias_x: bfloat16 [1536], P('head'), may hold values from -3 to 3
- bias_bc: bfloat16 [256], P('head'), may hold values from -3 to 3
- dt_bias: bfloat16 [24], P('head'), may hold values from -5 to -3
- a_log: bfloat16 [24], P('head'), may hold values from -12 to 1
- d_skip: bfloat16 [24], P('head'), may hold values from 0.5 to 1.5
- gate_gain: bfloat16 [1536], P('head'), may hold values from 0.5 to 1.5
- proj_out: bfloat16 [1536, 768], P('head'), may hold values from -0.15625 to 0.15625
Outputs:
- block_out: bfloat16 [4, 2048, 768], P(None, 'seq', 'head')
- in_grad: float32 [4, 2048, 768], P(None, 'seq', 'head')
- grad_norm_gain: float32 [768], P('head')
- grad_proj_z: float32 [768, 1536], P(None, 'head')
- grad_proj_x: float32 [768, 1536], P(None, 'head')
- grad_proj_bc: float32 [768, 256], P(None, 'head')
- grad_proj_dt: float32 [768, 24], P(None, 'head')
- grad_conv_x: float32 [4, 1536], P(None, 'head')
- grad_conv_bc: float32 [4, 256], P(None, 'head')
- grad_bias_x: float32 [1536], P('head')
- grad_bias_bc: float32 [256], P('head')
- grad_dt_bias: float32 [24], P('head')
- grad_a_log: float32 [24], P('head')
- grad_d_skip: float32 [24], P('head')
- grad_gate_gain: float32 [1536], P('head')
- grad_proj_out: float32 [1536, 768], P('head')
Inputs may be any that keep to these rules, and one draw needn't show every extreme that they name: Each row holds 4 lengths that sum to 2048; exactly one of them is 2048 minus half of 256, the others share the rest.
All inputs are finite; a program needn't handle non-finite values.
Results may differ from a plain program's by a relative error of at most 0.012.
The roundings to bfloat16 on the way count: a program that leaves them out, or rounds other values in their place, can miss the bound.
Values may be sent and summed in bfloat16 or wider, within the bound.
No kernel may reach another device: no remote copies, remote signals or barrier semaphores. Data moves between devices by JAX's collectives and lax.ppermute only.
A program may use at most 192 MiB of HBM per device.

v0:
```python
import functools

import jax
import jax.numpy as jnp
from jax import lax
from jax.experimental import pallas as pl
from jax.experimental.pallas import tpu as pltpu
from jax.sharding import PartitionSpec as P

EPSILON = 1e-05
bf16 = jnp.bfloat16
f32 = jnp.float32
LANES = 128
EDGE = 16
MIB = 1024 * 1024
STEPS = 32000.0
UNIT = 16384.0
LN2 = 0.6931471805599453
GROUP = 16
SMALL = 32


def permuted(x, axis, route):
    y = lax.ppermute(x, axis, route)
    order.near.append(y)
    return y


def swap(x, axis, bit):
    return permuted(x, axis, [(i, i ^ bit) for i in range(lax.axis_size(axis))])


def shift(x, axis, distance):
    n = lax.axis_size(axis)
    return permuted(x, axis, [(i, i + distance) for i in range(n) if 0 <= i + distance < n])


def head_pieces(x):
    far = swap(x, "head", 2)
    near = swap(x, "head", 1)
    return x, near, far, swap(far, "head", 1)


def nn(a, b):
    return lax.dot_general(a, b, (((1,), (0,)), ((), ())), preferred_element_type=f32)


def nt(a, b):
    return lax.dot_general(a, b, (((1,), (1,)), ((), ())), preferred_element_type=f32)


def tn(a, b):
    return lax.dot_general(a, b, (((0,), (0,)), ((), ())), preferred_element_type=f32)


def split2(v):
    hi = v.astype(bf16)
    return hi, (v - hi.astype(f32)).astype(bf16)


def split3(v):
    hi = v.astype(bf16)
    rest = v - hi.astype(f32)
    mid = rest.astype(bf16)
    return hi, mid, (rest - mid.astype(f32)).astype(bf16)


def spread_matrix(heads, size):
    row = lax.broadcasted_iota(jnp.int32, (LANES, heads * size), 0)
    col = lax.broadcasted_iota(jnp.int32, (LANES, heads * size), 1)
    first = (col >= row * size) & (col < (row + 1) * size)
    again = (col >= (row - GROUP) * size) & (col < (row - GROUP + 1) * size)
    return jnp.where(first | again, 1.0, 0.0).astype(bf16)


def spread(v, matrix, heads):
    hi, lo = split2(head_lanes(v, heads))
    return nn((hi.astype(f32) + to_group(lo.astype(f32), 1)).astype(bf16), matrix)


def head_lanes(v, heads):
    return jnp.where(lax.broadcasted_iota(jnp.int32, v.shape, 1) < heads, v, 0.0)


def to_group(v, k):
    return pltpu.roll(v, k * GROUP, 1)


def from_group(v, k, heads):
    return head_lanes(pltpu.roll(v, LANES - k * GROUP, 1) if k else v, heads)


def collapse(v, matrix, heads):
    return head_lanes(nt(jnp.concatenate(split2(v), axis=1), jnp.concatenate([matrix] * 2, axis=1)), heads)


def triangle(count, lower):
    row = lax.broadcasted_iota(jnp.int32, (count, count), 0)
    col = lax.broadcasted_iota(jnp.int32, (count, count), 1)
    keep = (row >= col) if lower else (row <= col)
    return jnp.where(keep, 1.0, 0.0).astype(bf16)


def exact_sums(matrix, v, heads):
    hi, mid, lo = [piece.astype(f32) for piece in split3(v)]
    sums = nn(matrix, (hi + to_group(mid, 1) + to_group(lo, 2)).astype(bf16))
    return from_group(sums, 0, heads) + from_group(sums, 1, heads) + from_group(sums, 2, heads)


def step_sizes(v, heads):
    soft = jnp.maximum(v, 0.0) + jnp.log1p(jnp.exp(-jnp.abs(v)))
    return head_lanes(soft, heads)


def steps_of(block, heads):
    return step_sizes(block, heads), from_group(block, 1, heads)


def segments(positions, lens_ref, pack, count):
    total = jnp.zeros(positions.shape, jnp.int32)
    end = jnp.int32(0)
    for k in range(count):
        end = end + lens_ref[pack, k]
        total = total + jnp.where(positions >= end, 1, 0)
    return total


def column_segments(meta_ref, lens_ref, pack, count, nseq, before):
    rows = lax.broadcasted_iota(jnp.int32, (count + before, 1), 0)
    return segments(rows + (meta_ref[0] * count - before), lens_ref, pack, nseq)


def row_segments(meta_ref, lens_ref, pack, count, nseq):
    cols = lax.broadcasted_iota(jnp.int32, (1, count), 1)
    return segments(cols + meta_ref[0] * count, lens_ref, pack, nseq)


def carry_column(meta_ref, seg_ext, before):
    same = seg_ext[before:] == seg_ext[before - 1 : before]
    return jnp.where(same & (meta_ref[0] > 0), 1.0, 0.0)


def to_int16(v):
    return jnp.floor(v + 0.5).astype(jnp.int32).astype(jnp.int16)


def encode_state(out, p, state, decay, heads, size):
    lane = lax.broadcasted_iota(jnp.int32, (1, LANES), 1)
    powers = jnp.zeros((1, LANES), f32)
    for h in range(heads):
        part = state[h * size : (h + 1) * size]
        top = jnp.max(jnp.max(jnp.abs(part), axis=0, keepdims=True), axis=1, keepdims=True)
        power = jnp.ceil(jnp.log(jnp.maximum(top, 1e-30)) / LN2)
        powers = powers + jnp.where(lane == h, power, 0.0)
        codes = jnp.clip(part * (jnp.exp(-power * LN2) * STEPS), -32767.0, 32767.0)
        out[p, h * size : (h + 1) * size, :] = to_int16(codes)
    row = lax.broadcasted_iota(jnp.int32, (EDGE, LANES), 0)
    coarse = jnp.floor(decay * UNIT)
    fine = (decay * UNIT - coarse) * UNIT
    tail = jnp.where(row == 0, powers, jnp.where(row == 1, coarse, jnp.where(row == 2, fine, 0.0)))
    out[p, heads * size :, :] = to_int16(tail)


def decode_state(block, heads, size):
    values = block.astype(jnp.int32).astype(f32)
    tail = values[heads * size :]
    scale = jnp.exp(tail[0:1] * LN2) / STEPS
    decay = (tail[1:2] + tail[2:3] / UNIT) / UNIT
    return scaled_state(values[: heads * size], scale, heads, size), decay


def sigmoid(v):
    return 1.0 / (1.0 + jnp.exp(-v))


def scaled_state(state, decay, heads, size):
    return jnp.concatenate(
        [state[h * size : (h + 1) * size] * decay[:, h : h + 1] for h in range(heads)], axis=0
    )


def tail_kernel(meta, tokens, out):
    lane = lax.broadcasted_iota(jnp.int32, out.shape, 1)
    total = jnp.zeros(out.shape, f32)
    for p in range(tokens.shape[0]):
        moved = pltpu.roll(tokens[p].astype(f32), (p + 1) * EDGE, 1)
        total = jnp.where((lane >= p * EDGE) & (lane < (p + 1) * EDGE), moved, total)
    out[...] = total.astype(bf16)


def wide_row(ref, lanes=LANES):
    row = ref[...].astype(f32)[None, :]
    blank = lanes - row.shape[1]
    return jnp.concatenate([row, jnp.zeros((1, blank), f32)], axis=1) if blank else row


def prepare_kernel(dims, *refs):
    packs, count, features, inner, bc, heads, size, width, nseq = dims
    (
        wbc, conv_bc, bias_bc, norm_gain, wdt, conv_x, bias_x, dt_bias, a_log, d_skip, gate_gain, wout,
        wout_o, shared_o, wbc_o, wdt_o, wdt_rows_o, conv_x_o, conv_bc_o, small_o, skip_o, gate_gain_o, gain_o,
    ) = refs
    bc_part, part = bc // 4, features // 4
    wout_o[...] = jnp.transpose(wout[...])
    taps = conv_bc[...].astype(f32)
    bias = wide_row(bias_bc, bc_part)
    gain = wide_row(norm_gain, part)
    pieces = [gain[:, c * bc_part : (c + 1) * bc_part] for c in range(part // bc_part)]
    rows = jnp.concatenate([taps, bias] + pieces, axis=0)
    rows = jnp.concatenate([rows, jnp.zeros((LANES - rows.shape[0], bc_part), f32)], axis=0)
    rows = jnp.concatenate([rows, jnp.zeros((LANES, LANES - bc_part), f32)], axis=1)
    extra = jnp.transpose(rows)[:bc_part].astype(bf16)
    shared_o[:, :features] = wbc[...]
    shared_o[:, features:] = extra
    wbc_o[...] = jnp.transpose(wbc[...].astype(f32)).astype(bf16)
    dt_rows = jnp.concatenate(
        [wdt[...].astype(f32), jnp.zeros((LANES - heads, features), f32)], axis=0
    )
    wdt_rows_o[...] = dt_rows.astype(bf16)
    wdt_o[...] = jnp.transpose(dt_rows).astype(bf16)
    blank = jnp.zeros((7 - width, inner), f32)
    conv_x_o[...] = jnp.concatenate(
        [conv_x[...].astype(f32), wide_row(bias_x, inner), blank], axis=0
    )
    conv_bc_o[...] = jnp.concatenate([taps, bias, blank[:, :bc_part]], axis=0)
    small_o[...] = jnp.concatenate(
        [wide_row(dt_bias), wide_row(a_log), jnp.zeros((6, LANES), f32)], axis=0
    )
    skips = jnp.concatenate([wide_row(d_skip), jnp.zeros((7, LANES), f32)], axis=0)
    matrix = spread_matrix(heads, size)
    skip_o[...] = sum(nn(piece, matrix) for piece in split3(skips))[0:1]
    gate_gain_o[...] = wide_row(gate_gain, inner)
    column = jnp.concatenate([gain, jnp.zeros((LANES - 1, part), f32)], axis=0)
    column = jnp.concatenate([column, jnp.zeros((LANES, 2 * LANES - part), f32)], axis=1)
    gain_o[...] = jnp.transpose(column)[:part, 0:1]


def normalise(values, gain, features):
    mean = jnp.sum(values * values, axis=0, keepdims=True) / features
    inv = lax.rsqrt(mean + EPSILON)
    return inv, ((values * inv) * gain).astype(bf16)


def raw_rows(normed, wx, wbc):
    return jnp.concatenate([nn(normed, wx), nt(normed, wbc)], axis=1).astype(bf16)


def border_kernel(dims, meta, *refs):
    packs, count, features, inner, bc, heads, size, width, nseq = dims
    edges, shared = refs[0:4], refs[4:8]
    wx, conv_x, wbc_o, conv_o, gain_o, edge_o, raws_o, stage, weights = refs[8:]
    head = meta[1]
    part, bc_part = features // 4, bc // 4
    for k in range(4):
        weights[head ^ k] = shared[k][...]
        stage[head ^ k] = edges[k][...]
    whole = weights[...].reshape(bc, weights.shape[2])
    wbc_o[...] = whole[:, :features]
    extra = whole[:, features:].astype(f32)
    conv_o[:, :inner] = conv_x[...]
    conv_o[:, inner:] = jnp.transpose(extra)[0:8]
    for h in range(4):
        for c in range(part // bc_part):
            gain_o[h * part + c * bc_part : h * part + (c + 1) * bc_part, :] = extra[
                h * bc_part : (h + 1) * bc_part, width + 1 + c : width + 2 + c
            ]
    _, normed = normalise(stage[...].reshape(features, stage.shape[2]).astype(f32), gain_o[...], features)
    edge_o[...] = normed
    raws_o[...] = raw_rows(jnp.transpose(normed), wx[...], wbc_o[...]).astype(f32)


def front_kernel(dims, keep, meta, lens, *refs):
    packs, count, features, inner, bc, heads, size, width, nseq = dims
    tokens, refs = refs[0:4], refs[4:]
    wx, wbc, wdt, conv, small, gain, edge_raws, *refs = refs
    normed_o, inv_o, rawx_o, rawbc_o, xbc_o, steps_o, state_o, stage, raws = refs[-9:]
    side = meta[0] & 1 if keep else 1 - (meta[0] & 1)
    pack = order.pack + (packs // 2) * side
    head = meta[1]
    for k in range(4):
        stage[head ^ k] = tokens[k][0]
    inv, normed_t = normalise(stage[...].reshape(features, count).astype(f32), gain[...], features)
    inv_o[0] = inv
    normed_o[0] = normed_t
    normed = jnp.transpose(normed_t)
    raws[EDGE:, :] = raw_rows(normed, wx[...], wbc[...]).astype(f32)
    raws[0:EDGE, :] = edge_raws[pl.ds(pl.multiple_of(pack * EDGE, EDGE), EDGE), :]

    def own_bc(values):
        bc_part = bc // 4
        parts = [values[:, inner + h * bc_part : inner + (h + 1) * bc_part] for h in range(4)]
        low = jnp.where((head & 1) == 0, parts[0], parts[1])
        high = jnp.where((head & 1) == 0, parts[2], parts[3])
        return jnp.where((head >> 1) == 0, low, high)

    rawx_o[0] = raws[:, :inner].astype(bf16)
    rawbc_o[0] = own_bc(raws[...]).astype(bf16)
    seg = column_segments(meta, lens, pack, count, nseq, EDGE)
    seg_main = seg[EDGE:]
    pre = convolved(raws, conv, seg, count, width)
    xbc = (pre * sigmoid(pre)).astype(bf16)
    xbc_o[0] = xbc
    v = head_lanes(nt(normed, wdt[...]).astype(bf16).astype(f32) + small[0:1, :], heads)
    dt = step_sizes(v, heads)
    rate = -dt * jnp.exp(small[1:2, :])
    cum = exact_sums(triangle(count, True), rate, heads)
    steps_o[0] = v + to_group(cum, 1)
    cum_end = cum[count - 1 : count]
    weight = jnp.where(seg_main == seg[count + EDGE - 1 :], jnp.exp(cum_end - cum), 0.0) * dt
    matrix = spread_matrix(heads, size)
    scaled = (xbc[:, :inner].astype(f32) * spread(weight, matrix, heads)).astype(bf16)
    state = jnp.transpose(nn(jnp.transpose(xbc[:, inner : inner + bc // 2]), scaled))
    carry = carry_column(meta, seg, EDGE)
    encode_state(state_o, 0, state, carry[count - 1 :] * jnp.exp(cum_end), heads, size)


def convolved(raws, conv, seg, count, width):
    pre = jnp.broadcast_to(conv[width : width + 1, :], (count, raws.shape[1]))
    for k in range(width):
        low = EDGE - (width - 1) + k
        mask = jnp.where(seg[low : low + count] == seg[EDGE:], 1.0, 0.0)
        pre = pre + conv[k : k + 1, :] * raws[low : low + count, :] * mask
    return pre


def gate_slope_kernel(dims, meta, lens, *refs):
    packs, count, features, inner, bc, heads, size, width, nseq = dims
    normed, wz, raw_x, raw_bc, conv_x, conv_bc, gate_o, slope_x_o, slope_bc_o, raws, raws_bc = refs
    pack = order.pack
    gate_o[0] = tn(normed[0], wz[...]).astype(bf16)
    seg = column_segments(meta, lens, pack, count, nseq, EDGE)
    for raw, wide, conv, out in ((raw_x, raws, conv_x, slope_x_o), (raw_bc, raws_bc, conv_bc, slope_bc_o)):
        wide[...] = raw[0].astype(f32)
        pre = convolved(wide, conv, seg, count, width)
        sig = sigmoid(pre)
        out[0] = sig * (1.0 + pre * (1.0 - sig))


def store_state(meta, packs, pack, keep_o, send_o, state, decay, heads, size):
    mine = (pack // (packs // 2)) == (meta[0] & 1)

    @pl.when(mine)
    def _():
        encode_state(keep_o, 0, state, decay, heads, size)

    @pl.when(jnp.logical_not(mine))
    def _():
        encode_state(send_o, 0, state, decay, heads, size)


def load_state(meta, packs, pack, keep, recv, heads, size):
    mine = (pack // (packs // 2)) == (meta[0] & 1)
    block = jnp.where(mine, keep[0].astype(jnp.int32), recv[0].astype(jnp.int32))
    return decode_state(block, heads, size)[0]


def decay_parts(cum_col, cum_row, masked):
    return masked * jnp.exp(jnp.minimum(cum_col - cum_row, 0.0))


def block_mask(meta, lens, pack, count, nseq):
    col = column_segments(meta, lens, pack, count, nseq, 0)
    row = row_segments(meta, lens, pack, count, nseq)
    tri = lax.broadcasted_iota(jnp.int32, (count, count), 0) >= lax.broadcasted_iota(
        jnp.int32, (count, count), 1
    )
    return tri & (col == row)


def inner_kernel(dims, meta, lens, *refs):
    packs, count, features, inner, bc, heads, size, width, nseq = dims
    xbc, steps, inner_o = refs
    pack = order.pack
    half = bc // 2
    b_vals, c_vals = xbc[0, :, inner : inner + half], xbc[0, :, inner + half :]
    scores = jnp.where(block_mask(meta, lens, pack, count, nseq), nt(c_vals, b_vals), 0.0)
    dt, cum_col = steps_of(steps[0], heads)
    cum_row = jnp.transpose(cum_col)
    dt_row = jnp.transpose(dt)
    lane = lax.broadcasted_iota(jnp.int32, (count, 2 * size), 1)
    for pair in range(heads // 2):
        cols = slice(2 * pair * size, (2 * pair + 2) * size)
        x_pair = xbc[0, :, cols]
        parts = []
        for h in (2 * pair, 2 * pair + 1):
            weights = decay_parts(cum_col[:, h : h + 1], cum_row[h : h + 1], scores)
            parts.append(nn((weights * dt_row[h : h + 1]).astype(bf16), x_pair))
        inner_o[0, :, cols] = jnp.where(lane < size, parts[0], parts[1])


def cot_kernel(dims, meta, lens, *refs):
    packs, count, features, inner, bc, heads, size, width, nseq = dims
    pieces, (wout, cot_o, gg_o, stage) = refs[:4], refs[4:]
    for k in range(4):
        stage[meta[1] ^ k] = pieces[k][0]
    cotangent = stage[...].reshape(features, count)
    cot_o[0] = cotangent
    gg_o[0] = jnp.transpose(nn(wout[...], cotangent))


def compose(lower, upper, heads, size):
    return scaled_state(lower[0], upper[1], heads, size) + upper[0], lower[1] * upper[1]


def choose(flag, a, b):
    return jnp.where(flag, a[0], b[0]), jnp.where(flag, a[1], b[1])


def pair_kernel(dims, rev, meta, own, other, out):
    packs, heads, size = dims
    upper_is_own = ((meta[0] & 1) ^ rev) == 1
    for p in range(packs // 2):
        a, b = decode_state(own[p], heads, size), decode_state(other[p], heads, size)
        both = compose(choose(upper_is_own, b, a), choose(upper_is_own, a, b), heads, size)
        encode_state(out, p, *both, heads, size)


def entering_from(before, b, p, heads, size):
    if before is None:
        return (jnp.zeros_like(b[0]), jnp.ones_like(b[1])), b
    entering = decode_state(before[p], heads, size)
    return entering, compose(b, entering, heads, size)


def cube_kernel(dims, rev, bit, first, meta, *refs):
    packs, heads, size = dims
    total, other = refs[0], refs[1]
    before, next_o, before_o = (None, refs[2], refs[3]) if first else refs[2:5]
    upper_is_own = (((meta[0] >> bit) & 1) ^ rev) == 1
    for p in range(packs // 2):
        a, b = decode_state(total[p], heads, size), decode_state(other[p], heads, size)
        both = compose(choose(upper_is_own, b, a), choose(upper_is_own, a, b), heads, size)
        encode_state(next_o, p, *both, heads, size)
        entering, longer = entering_from(before, b, p, heads, size)
        encode_state(before_o, p, *choose(upper_is_own, longer, entering), heads, size)


def last_kernel(dims, rev, bit, first, meta, *refs):
    packs, heads, size = dims
    own, pair, other = refs[0:3]
    before, keep_o, send_o = (None, refs[3], refs[4]) if first else refs[3:6]
    add = (((meta[0] >> bit) & 1) ^ rev) == 1
    upper_is_own = ((meta[0] & 1) ^ rev) == 1
    for p in range(packs // 2):
        entering, longer = entering_from(
            before, decode_state(other[p], heads, size), p, heads, size
        )
        low = choose(add, longer, entering)
        lower = decode_state(jnp.where(upper_is_own, pair[p].astype(jnp.int32), own[p].astype(jnp.int32)), heads, size)
        high = compose(low, lower, heads, size)
        encode_state(keep_o, p, *choose(upper_is_own, high, low), heads, size)
        encode_state(send_o, p, *choose(upper_is_own, low, high), heads, size)


def gate_kernel(dims, meta, lens, *refs):
    packs, count, features, inner, bc, heads, size, width, nseq = dims
    xbc, steps, inner_in, keep, recv, gate, gg, gain, skip, y_o, stats_o = refs
    pack = order.pack
    state = jnp.concatenate(
        split2(load_state(meta, packs, pack, keep, recv, heads, size)), axis=1
    )
    carry = carry_column(meta, column_segments(meta, lens, pack, count, nseq, EDGE), EDGE)
    matrix = spread_matrix(heads, size)
    entering = spread(carry * jnp.exp(from_group(steps[0], 1, heads)), matrix, heads)
    c_vals = xbc[0, :, inner + bc // 2 :]
    y = inner_in[0] + entering * nt(jnp.concatenate([c_vals, c_vals], axis=1), state)
    y_o[0] = y
    gate_f = gate[0].astype(f32)
    ssd = y + xbc[0, :, :inner].astype(f32) * skip[...]
    mixed = ssd * (gate_f * sigmoid(gate_f))
    squares = jnp.sum(mixed * mixed, axis=1, keepdims=True)
    dots = jnp.sum(gain[...] * gg[0] * mixed, axis=1, keepdims=True)
    lane = lax.broadcasted_iota(jnp.int32, (count, LANES), 1)
    both = jnp.where(lane == 0, squares, 0.0) + jnp.where(lane == 1, dots, 0.0)
    stats_o[0] = jnp.transpose(both)[0:2]


def grad_kernel(dims, total_inner, meta, lens, *refs):
    packs, count, features, inner, bc, heads, size, width, nseq = dims
    (
        stats, near, far, diagonal, xbc, steps, y, gate, gg, gain, skip,
        gy_o, gated_o, ggate_o, keep_o, send_o, small_o,
    ) = refs
    pack = order.pack

    @order.first
    def _():
        small_o[...] = jnp.zeros_like(small_o)

    sums = (stats[0] + near[0]) + (far[0] + diagonal[0])
    row = lax.broadcasted_iota(jnp.int32, (LANES, count), 0)
    wide = jnp.where(row == 0, sums[0:1], 0.0) + jnp.where(row == 1, sums[1:2], 0.0)
    cols = jnp.transpose(wide)
    inv = lax.rsqrt(cols[:, 0:1] / total_inner + EPSILON)
    dot = cols[:, 1:2] / total_inner
    x_f, gg_f, gate_f = xbc[0, :, :inner].astype(f32), gg[0], gate[0].astype(f32)
    ssd = y[0] + x_f * skip[...]
    sig = sigmoid(gate_f)
    act = gate_f * sig
    mixed = ssd * act
    scaled = mixed * inv
    gated_o[0] = (scaled * gain[...]).astype(bf16)
    grad_mixed = inv * gain[...] * gg_f - mixed * (inv * inv * inv * dot)
    gy_f = grad_mixed * act
    gy_o[0] = gy_f
    ggate_o[0] = (grad_mixed * ssd * sig * (1.0 + gate_f * (1.0 - sig))).astype(bf16)
    carry = carry_column(meta, column_segments(meta, lens, pack, count, nseq, EDGE), EDGE)
    cum = from_group(steps[0], 1, heads)
    entering = carry * jnp.exp(cum)
    ey_hi, ey_lo = split2(gy_f * spread(entering, spread_matrix(heads, size), heads))
    c_rows = jnp.transpose(xbc[0, :, inner + bc // 2 :])
    state_grad = jnp.transpose(nn(c_rows, ey_hi) + nn(c_rows, ey_lo))
    small_o[0:1, :] += jnp.sum(gg_f * scaled, axis=0, keepdims=True)
    small_o[1:2, :] += jnp.sum(gy_f * x_f, axis=0, keepdims=True)
    return lambda: store_state(
        meta, packs, pack, keep_o, send_o, state_grad, entering[count - 1 :], heads, size
    )


def diag_kernel(dims, meta, lens, *refs):
    packs, count, features, inner, bc, heads, size, width, nseq = dims
    xbc, steps, gy, y, keep, recv, dx_o, dbc_o, sums_o = refs
    pack = order.pack
    half = bc // 2
    b_vals, c_vals = xbc[0, :, inner : inner + half], xbc[0, :, inner + half :]
    col = column_segments(meta, lens, pack, count, nseq, 0)
    row = row_segments(meta, lens, pack, count, nseq)
    mask = (col == row) & (
        lax.broadcasted_iota(jnp.int32, (count, count), 0)
        <= lax.broadcasted_iota(jnp.int32, (count, count), 1)
    )
    scores = jnp.where(mask, nt(b_vals, c_vals), 0.0)
    dt, cum_col = steps_of(steps[0], heads)
    cum_row = jnp.transpose(cum_col)
    lane = lax.broadcasted_iota(jnp.int32, (count, 2 * size), 1)
    grad_scores = jnp.zeros((count, count), f32)
    zero = jnp.zeros((), bf16)
    for pair in range(heads // 2):
        cols = slice(2 * pair * size, (2 * pair + 2) * size)
        x_pair = xbc[0, :, cols]
        x_twice = jnp.concatenate([x_pair, x_pair], axis=1)
        gy_hi, gy_lo = split2(gy[0, :, cols])
        gy_wide = jnp.concatenate([gy_hi, gy_lo], axis=1)
        parts = []
        for h in (2 * pair, 2 * pair + 1):
            own = (lane < size) if h % 2 == 0 else (lane >= size)
            part = jnp.exp(jnp.minimum(cum_row[h : h + 1] - cum_col[:, h : h + 1], 0.0)) * dt[:, h : h + 1]
            parts.append(nn((scores * part).astype(bf16), gy_wide))
            both = jnp.concatenate([jnp.where(own, gy_hi, zero), jnp.where(own, gy_lo, zero)], axis=1)
            grad_scores = grad_scores + nt(x_twice, both) * part
        two = [part[:, : 2 * size] + part[:, 2 * size :] for part in parts]
        dx_o[0, :, cols] = jnp.where(lane < size, two[0], two[1])
    hi, lo = split2(jnp.where(mask, grad_scores, 0.0))
    state_hi, state_lo = split2(load_state(meta, packs, pack, keep, recv, heads, size))
    carry = carry_column(meta, column_segments(meta, lens, pack, count, nseq, EDGE), EDGE)
    matrix = spread_matrix(heads, size)
    ey_hi, ey_lo = split2(gy[0] * spread(carry * jnp.exp(cum_col), matrix, heads))
    dbc_o[0, :, :half] = nn(
        jnp.concatenate([hi, lo], axis=1), jnp.concatenate([c_vals, c_vals], axis=0)
    )
    b_rows = jnp.transpose(b_vals)
    dbc_o[0, :, half:] = (
        jnp.transpose(nn(b_rows, hi) + nn(b_rows, lo))
        + nn(ey_hi, state_hi) + nn(ey_hi, state_lo) + nn(ey_lo, state_hi)
    )
    row_sum = collapse(gy[0] * y[0], matrix, heads)
    col_sum = collapse(xbc[0, :, :inner].astype(f32) * dx_o[0], matrix, heads)
    sums_o[0] = row_sum + to_group(col_sum, 1)


def scatter_pieces(head, stage, own_o, far_o, send_o):
    own_o[0] = stage[head]
    send_o[0, 0] = stage[head ^ 1].astype(bf16)
    far_o[0] = stage[head ^ 2]
    send_o[0, 1] = stage[head ^ 3].astype(bf16)


def accumulate(meta, pack, packs, sums, term, keep_o, send_o):
    sums[...] += term.reshape(sums.shape)

    def finish():
        @last_pack(pack, packs)
        def _():
            side = meta[0] & 1
            keep_o[...] = sums[side]
            send_o[...] = sums[1 - side].astype(bf16)

    return finish


def last_pack(pack, packs):
    return lambda work: pl.when(pack == packs - 1)(work)


def cleared(*refs):
    @order.first
    def _():
        for ref in refs:
            ref[...] = jnp.zeros_like(ref)


def out_kernel(dims, meta, lens, *refs):
    packs, count, features, inner, bc, heads, size, width, nseq = dims
    gated, cot, wout, own_o, far_o, send_o, keep_o, give_o, stage, sums = refs
    pack = order.pack
    cleared(sums)
    stage[...] = nt(wout[...], gated[0]).reshape(stage.shape)
    scatter_pieces(meta[1], stage, own_o, far_o, send_o)
    return accumulate(meta, pack, packs, sums, nn(cot[0], gated[0]), keep_o, give_o)


def gain_row(weights, grads):
    part = jnp.sum(weights.astype(f32) * grads, axis=1, keepdims=True)
    return jnp.transpose(jnp.broadcast_to(part, (part.shape[0], LANES)))[0:8]


def z_kernel(dims, meta, lens, *refs):
    normed, ggate, wz, keep_o, give_o, gain_o, sums = refs
    pack = order.pack
    cleared(sums)
    store = accumulate(meta, pack, dims[0], sums, nn(normed[0], ggate[0]), keep_o, give_o)

    def finish():
        store()

        @last_pack(pack, dims[0])
        def _():
            gain_o[...] = gain_row(wz[...], sums[...].reshape(wz.shape))

    return finish


def end_weights(seg, seg_main, cum_col, dt_col, count):
    cum_end = cum_col[count - 1 :]
    end = seg[count + EDGE - 1 :]
    return jnp.where(seg_main == end, jnp.exp(cum_end - cum_col), 0.0) * dt_col


def share_kernel(dims, meta, lens, *refs):
    packs, count, features, inner, bc, heads, size, width, nseq = dims
    (
        xbc, steps, dbc, gkeep, grecv, gy, dx, slope, conv, skip,
        own_o, near_o, grad_o, state_sum_o, edge_o,
        gpad,
    ) = refs
    pack = order.pack
    half, quarter = bc // 2, bc // 4
    g_hi, g_lo = split2(load_state(meta, packs, pack, gkeep, grecv, heads, size))
    seg = column_segments(meta, lens, pack, count, nseq, EDGE)
    dt, cum = steps_of(steps[0], heads)
    matrix = spread_matrix(heads, size)
    wide = spread(end_weights(seg, seg[EDGE:], cum, dt, count), matrix, heads)
    x_f = xbc[0, :, :inner].astype(f32)
    hi, lo = split2(wide * x_f)
    grad_b = dbc[0, :, :half] + nn(hi, g_hi) + nn(lo, g_hi) + nn(hi, g_lo)
    grad_c = dbc[0, :, half:]
    even = jnp.concatenate([grad_b[:, :quarter], grad_c[:, :quarter]], axis=1)
    odd = jnp.concatenate([grad_b[:, quarter:], grad_c[:, quarter:]], axis=1)
    first = (meta[1] & 1) == 0
    own_o[0] = jnp.where(first, even, odd)
    near_o[0] = jnp.where(first, odd, even)
    b_vals = xbc[0, :, inner : inner + half]
    u_wide = wide * nt(
        jnp.concatenate([b_vals, b_vals], axis=1), jnp.concatenate([g_hi, g_lo], axis=1)
    )
    state_sum_o[0] = collapse(x_f * u_wide, matrix, heads)
    grad_x = (dx[0] + u_wide + gy[0] * skip[...]) * slope[0]
    grad_o[0] = grad_x
    gpad[:EDGE, :] = jnp.zeros((EDGE, inner), f32)
    gpad[EDGE:, :] = grad_x[:EDGE]
    edge_o[0] = conv_rows(gpad, conv, seg, EDGE, width).astype(bf16)


def middle_kernel(dims, meta, *refs):
    packs, quarter = dims
    own, near, keep_o, send_o = refs
    half = packs // 2
    first = (meta[1] >> 1) == 0
    for p in range(half):
        a, b = own[p] + near[p], own[p + half] + near[p + half]
        low = jnp.concatenate([a[:, :quarter], b[:, :quarter]], axis=1)
        high = jnp.concatenate([a[:, quarter:], b[:, quarter:]], axis=1)
        keep_o[p] = jnp.where(first, low, high)
        send_o[p] = jnp.where(first, high, low)


def conv_taps(grads, raws, gconv_o, seg, count, width):
    seg_main = seg[EDGE : EDGE + count]
    for k in range(width):
        low = EDGE - (width - 1) + k
        mask = jnp.where(seg[low : low + count] == seg_main, 1.0, 0.0)
        gconv_o[k : k + 1, :] += jnp.sum(
            grads * (raws[low : low + count, :] * mask), axis=0, keepdims=True
        )
    gconv_o[width : width + 1, :] += jnp.sum(grads, axis=0, keepdims=True)


def conv_rows(gpad, conv, seg, rows, width):
    total = jnp.zeros((rows, gpad.shape[1]), f32)
    for lag in range(width):
        mask = jnp.where(seg[lag : lag + rows] == seg[:rows], 1.0, 0.0)
        k = width - 1 - lag
        total = total + conv[k : k + 1, :] * (gpad[lag : lag + rows, :] * mask)
    return total


def step_kernel(dims, meta, lens, *refs):
    packs, count, features, inner, bc, heads, size, width, nseq = dims
    (
        steps, sums, state_sums, keep, recv, gkeep, grecv, small, normed, wdt,
        gdt_o, gdt_rows_o, gsmall_o, gain_o,
        gdt_sums,
    ) = refs
    group, half = pl.program_id(0), packs // 2
    matrix = spread_matrix(heads, size)
    ones = jnp.ones((8, LANES), bf16)
    decay_rate = -jnp.exp(small[1:2, :])
    upper = triangle(count, False)
    rows = lax.broadcasted_iota(jnp.int32, (count, LANES), 0)
    mine = group == (meta[0] & 1)
    bias_sum, rate_sum = jnp.zeros((1, LANES), f32), jnp.zeros((1, LANES), f32)
    term = jnp.zeros((features, LANES), f32)
    for j in range(half):
        pick = lambda a, b: jnp.where(mine, a[j].astype(jnp.int32), b[j].astype(jnp.int32))
        state = decode_state(pick(keep, recv), heads, size)[0]
        gstate = decode_state(pick(gkeep, grecv), heads, size)[0]
        seg = column_segments(meta, lens, group * half + j, count, nseq, EDGE)
        v = steps[j]
        dt, cum = steps_of(v, heads)
        sig = head_lanes(sigmoid(v), heads)
        row_sum, col_sum = from_group(sums[j], 0, heads), from_group(sums[j], 1, heads)
        state_sum = state_sums[j]
        carry = carry_column(meta, seg, EDGE)
        hi, lo = split2(gstate * state)
        by_head = collapse(nt(ones, hi) + nt(ones, lo), matrix, heads)[0:1]
        last = by_head * carry[count - 1 :] * jnp.exp(cum[count - 1 :]) + jnp.sum(
            state_sum, axis=0, keepdims=True
        )
        grad_cum = row_sum - col_sum - state_sum + jnp.where(rows == count - 1, last, 0.0)
        grad_rate = exact_sums(upper, grad_cum, heads)
        ratio = jnp.where(dt > 1e-30, sig / jnp.maximum(dt, 1e-30), 1.0)
        grad_dt = head_lanes(ratio * (col_sum + state_sum) + grad_rate * decay_rate * sig, heads)
        low = grad_dt.astype(bf16)
        gdt_o[j] = low
        bias_sum = bias_sum + jnp.sum(grad_dt, axis=0, keepdims=True)
        rate_sum = rate_sum + jnp.sum(grad_rate * dt * decay_rate, axis=0, keepdims=True)
        term = term + nn(normed[j], low)

    @pl.when(group == 0)
    def _():
        gsmall_o[...] = jnp.zeros_like(gsmall_o)
        gdt_sums[...] = jnp.zeros_like(gdt_sums)

    gsmall_o[0:1, :] += bias_sum
    gsmall_o[1:2, :] += rate_sum
    gdt_sums[...] += term

    @pl.when(group == packs // half - 1)
    def _():
        gdt_rows_o[...] = jnp.transpose(gdt_sums[...])[0:8]
        gain_o[...] = gain_row(wdt[...], gdt_sums[...])


def xback_kernel(dims, meta, lens, *refs):
    packs, count, features, inner, bc, heads, size, width, nseq = dims
    (
        grads, raw, normed, edge, edge_x, conv, wx,
        main_o, keep_o, give_o, gconv_o, gain_o,
        gpad, raws, sums, rows_x,
    ) = refs
    pack = order.pack
    seg = column_segments(meta, lens, pack, count, nseq, EDGE)

    cleared(gconv_o, rows_x, sums)
    raws[...] = raw[0].astype(f32)
    gpad[:count, :] = grads[0]
    gpad[count:, :] = jnp.zeros((EDGE, inner), f32)
    conv_taps(grads[0], raws, gconv_o, seg, count, width)
    seg_pad = jnp.concatenate([seg[EDGE:], jnp.full((8, 1), -1, jnp.int32)], axis=0)
    main = conv_rows(gpad, conv, seg_pad, count, width).astype(bf16)
    main_o[0] = main
    rows_x[pl.ds(pl.multiple_of(pack * EDGE, EDGE), EDGE), :] = edge_x[0]
    sums[...] += nn(normed[0], main).reshape(sums.shape)

    def finish():
        @last_pack(pack, packs)
        def _():
            sums[...] += nn(edge[...], rows_x[...]).reshape(sums.shape)
            side = meta[0] & 1
            keep_o[...] = sums[side]
            give_o[...] = sums[1 - side].astype(bf16)
            gain_o[...] = gain_row(wx[...], sums[...].reshape(wx.shape))

    return finish


def conv_bc_kernel(dims, meta, lens, *refs):
    packs, count, features, inner, bc, heads, size, width, nseq = dims
    (
        keep, recv, slope, raw, normed, edge, wbc, conv, edge_x,
        gconv_x, gdt_rows, gsmall, gate_small, gain_z, gain_x, gain_dt, gain,
        rows_o, edges_o, give_o, small_o,
        gpad, raws, sums, edge_bc, gconv,
    ) = refs
    pack = order.pack
    quarter = bc // 4

    cleared(gconv, edge_bc, sums)
    gpad[:EDGE, :] = jnp.zeros((EDGE, quarter), f32)
    gpad[EDGE + count :, :] = jnp.zeros((EDGE, quarter), f32)
    both = keep[0] + recv[0]
    grad = jnp.where(pack < packs // 2, both[:, :quarter], both[:, quarter:]) * slope[0]
    seg = column_segments(meta, lens, pack, count, nseq, EDGE)
    raws[...] = raw[0].astype(f32)
    gpad[EDGE : EDGE + count, :] = grad
    conv_taps(grad, raws, gconv, seg, count, width)
    seg_pad = jnp.concatenate([seg, jnp.full((8, 1), -1, jnp.int32)], axis=0)
    grad_raw = conv_rows(gpad, conv, seg_pad, count + EDGE, width).astype(bf16)
    rows_o[0] = grad_raw[EDGE:]
    edge_bc[pl.ds(pl.multiple_of(pack * EDGE, EDGE), EDGE), :] = grad_raw[:EDGE]
    edges_o[0, :, :inner] = edge_x[0]
    blank = jnp.zeros((EDGE, LANES - quarter), bf16)
    edges_o[0, :, inner:] = jnp.concatenate([grad_raw[:EDGE], blank], axis=1)
    sums[...] += nn(normed[0], grad_raw[EDGE:])

    def finish():
        @last_pack(pack, packs)
        def _():
            total = sums[...] + nn(edge[...], edge_bc[...])
            rows = jnp.transpose(total)
            taps = width + 1
            give_o[:quarter, :] = rows[:, :inner].astype(bf16)
            give_o[quarter : 2 * quarter, :] = rows[:, inner:].astype(bf16)
            small_o[...] = jnp.zeros_like(small_o)
            for h in range(heads):
                small_o[2 * h : 2 * h + 1, :] = gdt_rows[h : h + 1, :inner]
                small_o[2 * h + 1 : 2 * h + 2, :] = gdt_rows[h : h + 1, inner:]
            row = 2 * heads
            small_o[row : row + taps, :] = gconv_x[:taps, :]
            row += taps
            small_o[row : row + 1, :] = gate_small[0:1, :]
            skips = collapse(gate_small[...], spread_matrix(heads, size), heads)
            small_o[row + 1 : row + 2, :] = jnp.concatenate(
                [gsmall[0:1, :], gsmall[1:2, :], skips[1:2, :]], axis=1
            )
            blank_row = jnp.zeros((1, inner - taps * quarter), f32)
            small_o[row + 2 : row + 3, :] = jnp.concatenate(
                [gconv[k : k + 1, :] for k in range(taps)] + [blank_row], axis=1
            )
            gains = gain_row(wbc[...], total)[0:1] + gain_z[0:1, :] + gain_x[0:1, :] + gain_dt[0:1, :]
            gains = gains / jnp.transpose(jnp.broadcast_to(gain[...], (features, LANES)))[0:1]
            small_o[row + 3 : row + 4, :] = gains[:, :inner]
            small_o[row + 4 : row + 5, :] = gains[:, inner:]
            hi, lo = split2(small_o[...])
            give_o[2 * quarter : 2 * quarter + SMALL, :] = hi
            give_o[2 * quarter + SMALL :, :] = lo

    return finish


def back_kernel(dims, meta, lens, *refs):
    packs, count, features, inner, bc, heads, size, width, nseq = dims
    (
        main, edges, ggate, gdt, gbc, normed, wz, wx, wbc, wdt,
        own_o, far_o, send_o, dots_o,
        stage,
    ) = refs
    head = meta[1]
    part, quarter = features // 4, bc // 4
    late = count - EDGE

    def with_edge(rows, edge):
        low = (rows[late:].astype(f32) + edge.astype(f32)).astype(bf16)
        return jnp.concatenate([rows[:late], low], axis=0)

    grad_x = with_edge(main[0], edges[0, :, :inner])
    grad_bc = with_edge(gbc[0], edges[0, :, inner : inner + quarter])
    whole = nt(wz[...], ggate[0]) + nt(wx[...], grad_x) + nt(wbc[...], grad_bc) + nt(wdt[...], gdt[0])
    dots = jnp.sum(whole * normed[0].astype(f32), axis=0, keepdims=True)
    stage[...] = whole.reshape(stage.shape)
    dots_o[0] = dots
    own_o[0] = stage[head]
    far_o[0] = stage[head ^ 2]
    for k in range(2):
        send_o[0, k, :part, :] = stage[head ^ (1 + 2 * k)].astype(bf16)
        send_o[0, k, part:, :] = extra_rows(dots)


def extra_rows(*values):
    row = lax.broadcasted_iota(jnp.int32, (EDGE, values[0].shape[1]), 0)
    total = jnp.zeros(row.shape, f32)
    for i, value in enumerate(values):
        for k, piece in enumerate(split3(value)):
            total = total + jnp.where(row == 3 * i + k, piece.astype(f32), 0.0)
    return total.astype(bf16)


def read_extra(block, i):
    rows = block.astype(f32)
    return rows[3 * i : 3 * i + 1] + rows[3 * i + 1 : 3 * i + 2] + rows[3 * i + 2 : 3 * i + 3]


def gather_kernel(own, far, near, dots, own_o, far_o, dots_o):
    part = own.shape[1]
    own_o[0] = own[0] + near[0, 0, :part, :].astype(f32)
    far_o[0, :part, :] = (far[0] + near[0, 1, :part, :].astype(f32)).astype(bf16)
    both = dots[0] + read_extra(near[0, 0, part:, :], 0)
    dots_o[0] = both
    far_o[0, part:, :] = extra_rows(both)


def final_kernel(dims, own, far, dots, tokens, inv, gain, out_grad, in_grad_o):
    packs, count, features = dims
    part = own.shape[1]
    grad = own[0] + far[0, :part, :].astype(f32)
    mean = (dots[0] + read_extra(far[0, part:, :], 0)) / features
    unit = tokens[0].astype(f32) * inv[0]
    in_grad_o[0] = out_grad[0].astype(f32) + inv[0] * (gain[...] * grad - unit * mean)


def out_gather_kernel(own, far, near, own_o, far_o):
    own_o[0] = own[0] + near[0, 0].astype(f32)
    far_o[0] = (far[0] + near[0, 1].astype(f32)).astype(bf16)


def out_final_kernel(own, far, tokens, out):
    out[0] = (tokens[0].astype(f32) + (own[0] + far[0].astype(f32))).astype(bf16)


def add_kernel(bit, halve, segs, count, small, meta, *refs):
    keep, got, refs = refs[:count], refs[count : 2 * count], refs[2 * count :]
    end = segs[-1] if count > 1 else sum(segs)
    write = 0
    if small:
        small_in, *refs, small_o = refs
        hi, lo = split2(small_in[...])
        mine = hi.astype(f32) + lo.astype(f32)
        theirs = got[-1][end : end + SMALL, :].astype(f32) + got[-1][end + SMALL :, :].astype(f32)
        total = mine + theirs
        small_o[...] = total
        if bit is not None:
            send_o = refs[-1]
            behind = send_o.shape[0] - 2 * SMALL
            hi, lo = split2(total)
            send_o[behind : behind + SMALL, :] = hi
            send_o[behind + SMALL :, :] = lo
    read = 0
    for i, rows in enumerate(segs):
        if count > 1:
            total = keep[i][...] + got[i][:rows, :].astype(f32)
        else:
            total = keep[0][read : read + rows, :].astype(f32) + got[0][read : read + rows, :].astype(f32)
        read += rows
        if halve:
            half = rows // 2
            first = ((meta[0] >> bit) & 1) == 0
            top, bottom = total[:half], total[half:]
            refs[0][write : write + half, :] = jnp.where(first, top, bottom)
            refs[1][write : write + half, :] = jnp.where(first, bottom, top).astype(bf16)
            write += half
        else:
            refs[0][write : write + rows, :] = total.astype(bf16)
            write += rows


def whole_kernel(quarter, keep, got, small, out, small_o):
    total = keep[: 2 * quarter, :].astype(f32) + got[: 2 * quarter, :].astype(f32)
    out[...] = jnp.concatenate([total[:quarter], total[quarter:]], axis=1)
    hi, lo = split2(small[...])
    end = 2 * quarter
    theirs = got[end : end + SMALL, :].astype(f32) + got[end + SMALL :, :].astype(f32)
    small_o[...] = (hi.astype(f32) + lo.astype(f32)) + theirs


def join_kernel(bit, segs, meta, mine, got, out):
    first = ((meta[0] >> bit) & 1) == 0
    read = 0
    for rows in segs:
        a = mine[read : read + rows, :].astype(f32)
        b = got[read : read + rows, :].astype(f32)
        out[2 * read : 2 * read + rows, :] = jnp.where(first, a, b).astype(bf16)
        out[2 * read + rows : 2 * read + 2 * rows, :] = jnp.where(first, b, a).astype(bf16)
        read += rows


def result_kernel(segs, ways, meta, mine, got, *outs):
    first = (meta[0] & 1) == 0
    read = 0
    for rows, way, out in zip(segs, ways, outs):
        a = mine[read : read + rows, :].astype(f32)
        b = got[read : read + rows, :].astype(f32)
        top, bottom = jnp.where(first, a, b), jnp.where(first, b, a)
        if way == "rows":
            out[:rows, :] = top
            out[rows:, :] = bottom
        elif way == "flip":
            out[:, :rows] = jnp.transpose(top)
            out[:, rows:] = jnp.transpose(bottom)
        else:
            out[...] = jnp.concatenate([top, bottom], axis=1)
        read += rows


def plus_kernel(a, b, out):
    out[...] = a[...] + b[...]


def unpack_kernel(dims, meta, *refs):
    heads, features, bc_part, width = dims
    smalls, gains, dt_o, taps_x_o, taps_bc_o, bias_x_o, bias_bc_o, dt_bias_o, a_log_o, skip_o, gate_o, gain_o = refs
    for h in range(heads):
        dt_o[h : h + 1, :] = jnp.concatenate(
            [smalls[2 * h : 2 * h + 1, :], smalls[2 * h + 1 : 2 * h + 2, :]], axis=1
        )
    row = 2 * heads
    taps_x_o[...] = smalls[row : row + width, :]
    bias_x_o[...] = smalls[row + width, :]
    row += width + 1
    gate_o[...] = smalls[row, :]
    for k, out in enumerate((dt_bias_o, a_log_o, skip_o)):
        out[...] = smalls[row + 1, k * LANES : k * LANES + heads]
    taps = smalls[row + 2 : row + 3, :]
    for k in range(width):
        taps_bc_o[k : k + 1, :] = taps[:, k * bc_part : (k + 1) * bc_part]
    bias_bc_o[...] = taps[0, width * bc_part : (width + 1) * bc_part]
    both = jnp.concatenate([gains[row + 3 : row + 4, :], gains[row + 4 : row + 5, :]], axis=1)
    part = features // 4
    parts = [both[:, h * part : (h + 1) * part] for h in range(4)]
    low = jnp.where((meta[1] & 1) == 0, parts[0], parts[1])
    high = jnp.where((meta[1] & 1) == 0, parts[2], parts[3])
    gain_o[...] = jnp.where((meta[1] >> 1) == 0, low, high)[0]


class Spec:
    def __init__(self, shape, index, each=True):
        self.shape, self.index, self.each = tuple(shape), index, each

    def block(self, group):
        zeros = (0,) * len(self.shape)
        if not self.each:
            return pl.BlockSpec(self.shape, lambda p, *_: zeros)
        size = group or 1
        return pl.BlockSpec(
            (size,) + self.shape, lambda p, *pre: (self.index(p, pre, bool(group)),) + zeros
        )


def whole_spec(shape):
    return Spec(shape, None, False)


def pack_spec(shape):
    return Spec(shape, lambda p, pre, grouped: p)


def half_spec(shape, half):
    return Spec(shape, lambda p, pre, grouped: 0 if grouped else p % half)


def sided_spec(shape, half, keep):
    def index(p, pre, grouped):
        side = pre[0][0] & 1 if keep else 1 - (pre[0][0] & 1)
        return side if grouped else p + half * side

    return Spec(shape, index)


def side_spec(shape, half, keep):
    def index(p, pre, grouped):
        if grouped:
            return 0
        side = pre[0][0] & 1 if keep else 1 - (pre[0][0] & 1)
        group = p // half
        return jnp.where(group == side, p % half, jnp.where(group < side, 0, half - 1))

    return Spec(shape, index)


class Each:
    def __init__(self, shape, dtype):
        self.shape, self.dtype = tuple(shape), dtype

    def scratch(self, group):
        return pltpu.VMEM(((group,) if group else ()) + self.shape, self.dtype)


class Order:
    def __init__(self):
        self.clear()

    def clear(self):
        self.last, self.near, self.held = (), [], []
        self.pack, self.lane, self.lanes = None, 0, 1

    def first(self, work):
        if self.lane == 0:
            pl.when(self.pack == 0)(work)

    def hold(self, *arrays):
        self.held += arrays

    def drop(self, *arrays):
        self.held = [x for x in self.held if not any(x is y for y in arrays)]

    def placed(self, x):
        return pltpu.with_memory_space_constraint(x, pltpu.VMEM) if self.holds(x) else x

    def holds(self, x):
        return any(x is y for y in self.near)


order = Order()


def call(
    kernel, grid, in_specs, out_specs, out_shape, scratch, prefetch, *args, limit=28, wait=(), us=1,
    out=False, onto=(), group=0,
):
    first = len(prefetch) + len(args)
    args = args + tuple(onto)
    in_specs = list(in_specs) + [pl.BlockSpec(memory_space=pl.ANY)] * len(onto)
    given = len(prefetch) + len(args)
    held = order.last + tuple(wait)
    held += tuple(x for x in order.held if not any(x is y for y in args + held))
    late = len(held)
    single = not isinstance(out_shape, (list, tuple))
    out_specs, out_shape = ([out_specs], [out_shape]) if single else (list(out_specs), list(out_shape))
    token = jax.ShapeDtypeStruct((8, LANES), f32)
    count = len(out_shape)
    results = count if out is True else int(out)

    specs = list(in_specs[: len(in_specs) - len(onto)]) + out_specs
    blocks = lambda items: [x.block(group) if isinstance(x, Spec) else x for x in items]

    def body(*refs):
        ins, rest = refs[:first], refs[given + late :]
        fixed, blocked = ins[: len(prefetch)], (*ins[len(prefetch) :], *rest[:count])
        own = rest[count + 1 :]
        finish = []
        for lane in range(group or 1):
            order.pack, order.lane, order.lanes = pl.program_id(0), lane, group or 1
            views, scratches = blocked, own
            if group:
                order.pack = order.pack * group + lane
                views = [
                    ref.at[pl.ds(lane, 1)] if isinstance(spec, Spec) and spec.each else ref
                    for ref, spec in zip(blocked, specs)
                ]
                scratches = [
                    ref.at[lane] if isinstance(item, Each) else ref for ref, item in zip(own, scratch)
                ]
            finish.append(kernel(*fixed, *views, *scratches))
        for work in finish:
            if work is not None:
                work()

    *outs, order_out = pl.pallas_call(
        body,
        grid_spec=pltpu.PrefetchScalarGridSpec(
            num_scalar_prefetch=len(prefetch),
            grid=grid,
            in_specs=blocks(in_specs) + [pl.BlockSpec(memory_space=pl.ANY)] * late,
            out_specs=blocks(out_specs + [whole_spec(token.shape)]),
            scratch_shapes=[x.scratch(group) if isinstance(x, Each) else x for x in scratch],
        ),
        input_output_aliases={first + i: i for i in range(len(onto))},
        out_shape=[
            x if i < results else pltpu.VMEM(x.shape, x.dtype) for i, x in enumerate(out_shape + [token])
        ],
        compiler_params=pltpu.CompilerParams(vmem_limit_bytes=limit * MIB),
        cost_estimate=pl.CostEstimate(
            flops=int(us * 10e9), bytes_accessed=int(us * 3e6), transcendentals=0
        ),
    )(*[pltpu.with_memory_space_constraint(x, pltpu.VMEM) for x in prefetch], *[order.placed(x) for x in args], *[order.placed(x) for x in held])
    order.last = (order_out,)
    order.near.append(order_out)
    order.near += outs[results:]
    return outs[0] if single else outs


def shape(*dims_and_type):
    return jax.ShapeDtypeStruct(dims_and_type[:-1], dims_and_type[-1])


def scan_states(keep, send, meta, packs, heads, size, rev, beside, waits=lambda: ()):
    dims = (packs, heads, size)
    rows = heads * size
    half = packs // 2
    pay = shape(half, rows + EDGE, LANES, jnp.int16)
    spec = whole_spec(pay.shape)
    bits = (lax.axis_size("seq") - 1).bit_length()
    beside = list(beside)

    def work(newest):
        if beside:
            beside.pop(0)(newest)

    other = swap(send, "seq", 1)
    work(send)
    keep = keep() if callable(keep) else keep
    total = call(
        functools.partial(pair_kernel, dims, rev), (1,), [spec, spec], spec, pay, [], (meta,),
        keep, other,
    )
    before = None
    for bit in range(1, bits):
        got = swap(total, "seq", 1 << bit)
        extra = () if before is None else (before,)
        work(total)
        if bit < bits - 1:
            total, before = call(
                functools.partial(cube_kernel, dims, rev, bit, before is None), (1,),
                [spec] * (2 + len(extra)), [spec, spec], [pay, pay], [], (meta,),
                total, got, *extra,
            )
        else:
            own, back = call(
                functools.partial(last_kernel, dims, rev, bit, before is None), (1,),
                [spec] * (3 + len(extra)), [spec, spec], [pay, pay], [],
                (meta,), keep, other, got, *extra, wait=waits(),
            )
    recv = swap(back, "seq", 1)
    while beside:
        work(back)
    return own, recv


class SeqSum:
    def __init__(self):
        self.keep, self.got, self.segs = [], [], []
        self.small = self.bit = None
        self.bits = list(range(1, (lax.axis_size("seq") - 1).bit_length()))
        self.halved = []

    def put(self, keep, give, segs=None, small=None):
        self.keep.append(keep)
        self.got.append(swap(give, "seq", 1))
        self.segs += segs or [keep.shape[0]]
        self.small = small

    def add(self, meta, us=1, wait=()):
        bit = self.bits.pop(0) if self.bits else None
        halve = bit is not None and all(rows % (2 * EDGE) == 0 for rows in self.segs)
        cols = self.keep[0].shape[1]
        segs = [rows // 2 for rows in self.segs] if halve else self.segs
        rows = sum(segs)
        small = self.small is not None
        behind = 2 * SMALL if small and bit is not None else 0
        low = shape(rows + behind, cols, bf16)
        out = [shape(rows, cols, f32), low] if halve else [low]
        ins = [*self.keep, *self.got]
        if small:
            ins.append(self.small)
            out.append(shape(*self.small.shape, f32))
        outs = call(
            functools.partial(add_kernel, bit, halve, self.segs, len(self.keep), small), (1,),
            [whole_spec(x.shape) for x in ins], [whole_spec(x.shape) for x in out], out, [],
            (meta,), *ins, us=us, wait=wait,
        )
        if small:
            self.small = outs[-1]
        self.segs, self.keep = segs, [outs[0]]
        if bit is None:
            return True
        self.got = [swap(outs[1] if halve else outs[0], "seq", 1 << bit)]
        if halve:
            self.halved.append(bit)
        return False

    def send_back(self):
        self.bit = self.halved.pop() if self.halved else 0
        self.got = [swap(self.keep[0], "seq", 1 << self.bit)]

    def join(self, meta, us=1):
        rows, cols = self.keep[0].shape
        both = shape(2 * rows, cols, bf16)
        spec = whole_spec((rows, cols))
        self.keep = [call(
            functools.partial(join_kernel, self.bit, self.segs), (1,), [spec, spec],
            whole_spec(both.shape), both, [], (meta,), self.keep[0], self.got[0], us=us,
        )]
        self.segs = [2 * rows for rows in self.segs]

    def result(self, meta, ways, us=0.01):
        cols = self.keep[0].shape[1]
        shapes = {"rows": lambda r: (2 * r, cols), "flip": lambda r: (cols, 2 * r), "cols": lambda r: (r, 2 * cols)}
        out = [shape(*shapes[way](rows), f32) for way, rows in zip(ways, self.segs)]
        spec = whole_spec(self.keep[0].shape)
        return call(
            functools.partial(result_kernel, self.segs, ways), (1,), [spec, spec],
            [whole_spec(x.shape) for x in out], out, [], (meta,), self.keep[0], self.got[0],
            out=True, us=us,
        )


def advance(total, meta, us=1, wait=()):
    if total.bit is None:
        if total.add(meta, us, wait):
            total.send_back()
    elif total.bit:
        total.join(meta, us)
        total.send_back()


def shards(
    tokens_in, out_grad, lengths, norm_gain, proj_z, proj_x, proj_bc, proj_dt, conv_x, conv_bc,
    bias_x, bias_bc, dt_bias, a_log, d_skip, gate_gain, proj_out,
):
    packs, count, part = tokens_in.shape
    features, inner = proj_x.shape
    heads = proj_dt.shape[1]
    size = inner // heads
    width = conv_x.shape[0]
    nseq = lengths.shape[1]
    bc_part = proj_bc.shape[1]
    bc = bc_part * lax.axis_size("head")
    half = packs // 2
    chans = inner + bc
    ext = count + EDGE
    rows = heads * size
    total_inner = inner * lax.axis_size("head")
    dims = (packs, count, features, inner, bc, heads, size, width, nseq)
    seq_place, head_place = lax.axis_index("seq"), lax.axis_index("head")
    meta = jnp.stack([seq_place, head_place]).astype(jnp.int32)
    pre = (meta, lengths)
    grid = (packs,)

    order.clear()
    tokens = jnp.swapaxes(tokens_in, 1, 2)
    cotangent = jnp.swapaxes(out_grad, 1, 2)
    far = swap(tokens, "head", 2)
    near = swap(tokens, "head", 1)
    tail = call(
        tail_kernel, (1,),
        [pl.BlockSpec((packs, part, LANES), lambda p, _: (0, 0, count // LANES - 1))],
        whole_spec((part, LANES)), shape(part, LANES, bf16), [], (meta,),
        pltpu.with_memory_space_constraint(tokens, pltpu.HBM), us=0.05,
    )
    tail = shift(tail, "seq", 1)
    ins = [
        proj_bc.T, conv_bc, bias_bc, norm_gain, proj_dt.T, conv_x, bias_x, dt_bias, a_log, d_skip,
        gate_gain, proj_out,
    ]
    outs = [
        shape(features, inner, bf16),
        shape(bc_part, features + LANES, bf16), shape(features, bc_part, bf16),
        shape(features, LANES, bf16), shape(LANES, features, bf16), shape(8, inner, f32),
        shape(8, bc_part, f32), shape(8, LANES, f32), shape(1, inner, f32), shape(1, inner, f32),
        shape(part, 1, f32),
    ]
    (
        w_out, shared, w_bc, w_dt, w_dt_rows, conv_own, conv_bc_own, small, skip, gain_gate, norm_gain_own,
    ) = call(
        functools.partial(prepare_kernel, dims), (1,), [whole_spec(x.shape) for x in ins],
        [whole_spec(x.shape) for x in outs], outs, [], (), *ins, wait=(tail,),
        us=0.05,
    )
    edge_far, shared_far = swap(tail, "head", 2), swap(shared, "head", 2)
    far, edge_far, shared_far = lax.optimization_barrier((far, edge_far, shared_far))
    edge_pieces = tail, swap(tail, "head", 1), edge_far, swap(edge_far, "head", 1)
    weight_pieces = shared, swap(shared, "head", 1), shared_far, swap(shared_far, "head", 1)
    diagonal = swap(far, "head", 1)
    token_pieces = tokens, near, far, diagonal

    lane_spec = pack_spec((count, LANES))
    chan_spec = pack_spec((count, inner))
    xbc_spec = pack_spec((count, chans))
    model_spec = pack_spec((features, count))
    piece_spec = pack_spec((part, count))
    edge_spec = whole_spec((part, LANES))
    pay_shape = (rows + EDGE, LANES)
    pay_specs = [side_spec(pay_shape, half, k) for k in (True, False)]
    pay = shape(half, *pay_shape, jnp.int16)
    state_spec = half_spec(pay_shape, half)
    vec = whole_spec((1, inner))
    square = whole_spec((features, inner))

    w_bc_rows, conv_all, gain_all, edge, edge_raws = call(
        functools.partial(border_kernel, dims),
        (1,),
        [edge_spec] * 4 + [whole_spec((bc_part, features + LANES))] * 4
        + [square, whole_spec((8, inner))],
        [
            whole_spec((bc, features)), whole_spec((8, chans)), whole_spec((features, 1)),
            whole_spec((features, LANES)), whole_spec((LANES, chans)),
        ],
        [
            shape(bc, features, bf16), shape(8, chans, f32), shape(features, 1, f32),
            shape(features, LANES, bf16), shape(LANES, chans, f32),
        ],
        [pltpu.VMEM((4, part, LANES), bf16), pltpu.VMEM((4, bc_part, features + LANES), bf16)],
        (meta,),
        *edge_pieces, *weight_pieces, proj_x, conv_own,
    )

    def front(keep, onto):
        spec = lambda shape_of: sided_spec(shape_of, half, keep)
        return call(
            functools.partial(front_kernel, dims, keep),
            (half,),
            [spec((part, count))] * 4
            + [
                square, whole_spec((bc, features)), whole_spec((LANES, features)),
                whole_spec((8, chans)), whole_spec((8, LANES)), whole_spec((features, 1)),
                whole_spec((LANES, chans)),
            ],
            [
                spec((features, count)), spec((1, count)), spec((ext, inner)), spec((ext, bc_part)),
                spec((count, chans)), spec((count, LANES)), pack_spec(pay_shape),
            ],
            [
                shape(packs, features, count, bf16), shape(packs, 1, count, f32),
                shape(packs, ext, inner, bf16), shape(packs, ext, bc_part, bf16),
                shape(packs, count, chans, bf16), shape(packs, count, LANES, f32), pay,
            ],
            [Each((4, part, count), bf16), Each((ext, chans), f32)],
            pre,
            *token_pieces, proj_x, w_bc_rows, w_dt_rows, conv_all, small, gain_all, edge_raws,
            us=6, onto=onto,
        )

    *early, send = front(False, ())
    kept = {}

    def keep_work(_):
        *kept["front"], kept["keep"] = front(True, early)
        order.hold(*(kept["front"][i] for i in (0, 4, 5)))

    def inner_work(_):
        *_, xbc, steps = kept["front"]
        kept["inner"] = call(
            functools.partial(inner_kernel, dims),
            grid,
            [xbc_spec, lane_spec],
            chan_spec,
            shape(packs, count, inner, f32),
            [],
            pre,
            xbc, steps,
            us=6,
        )
        order.hold(kept["inner"])

    def cot_work(newest):
        own, far = kept["cots"]
        near = swap(own, "head", 1)
        cots = own, near, far, swap(lax.optimization_barrier((far, newest))[0], "head", 1)
        kept["cot"], kept["gg"] = call(
            functools.partial(cot_kernel, dims),
            (packs // half,),
            [piece_spec] * 4 + [whole_spec((inner, features))],
            [model_spec, chan_spec],
            [shape(packs, features, count, bf16), shape(packs, count, inner, f32)],
            [Each((4, part, count), bf16)],
            pre,
            *cots, proj_out,
            us=5.5, group=half,
        )

    def gate_slope_work(_):
        normed, _, raw_x, raw_bc, *_ = kept["front"]
        own = lax.optimization_barrier((cotangent, normed))[0]
        kept["cots"] = own, swap(own, "head", 2)
        kept["slope"] = call(
            functools.partial(gate_slope_kernel, dims),
            grid,
            [model_spec, square, pack_spec((ext, inner)), pack_spec((ext, bc_part)),
             whole_spec((8, inner)), whole_spec((8, bc_part))],
            [chan_spec, chan_spec, pack_spec((count, bc_part))],
            [shape(packs, count, inner, bf16), shape(packs, count, inner, f32),
             shape(packs, count, bc_part, f32)],
            [Each((ext, inner), f32), Each((ext, bc_part), f32)],
            pre,
            normed, proj_z, raw_x, raw_bc, conv_own, conv_bc_own,
            us=7,
        )

    state_keep, state_recv = scan_states(
        lambda: kept["keep"], send, meta, packs, heads, size, 0,
        (keep_work, gate_slope_work, inner_work, cot_work),
    )
    normed, inv, raw_x, raw_bc, xbc, steps = kept["front"]
    inner_out, cot, gg = kept["inner"], kept["cot"], kept["gg"]
    gate, slope_x, slope_bc = kept["slope"]
    order.drop(inner_out)

    y, stats = call(
        functools.partial(gate_kernel, dims),
        (packs // half,),
        [
            xbc_spec, lane_spec, chan_spec, state_spec, state_spec, chan_spec, chan_spec, vec, vec,
        ],
        [chan_spec, pack_spec((2, count))],
        [shape(packs, count, inner, f32), shape(packs, 2, count, f32)],
        [],
        pre,
        xbc, steps, inner_out, state_keep, state_recv, gate, gg, gain_gate, skip,
        us=6.6, group=half,
    )
    stats = head_pieces(stats)

    gy, gated, ggate, gkeep, gsend, gate_small = call(
        functools.partial(grad_kernel, dims, total_inner),
        grid,
        [
            *[pack_spec((2, count))] * 4, xbc_spec, lane_spec, chan_spec, chan_spec, chan_spec, vec,
            vec,
        ],
        [chan_spec] * 3 + pay_specs + [whole_spec((8, inner))],
        [shape(packs, count, inner, f32)] + [shape(packs, count, inner, bf16)] * 2
        + [pay, pay, shape(8, inner, f32)],
        [],
        pre,
        *stats, xbc, steps, y, gate, gg, gain_gate, skip,
        us=8.3,
    )

    piece_shape = shape(packs, part, count, f32)
    send_spec = pack_spec((2, part, count))
    rows_half = features // 2
    half_specs = [whole_spec((rows_half, inner))] * 2
    half_shapes = [shape(rows_half, inner, f32), shape(rows_half, inner, bf16)]
    half_sums = pltpu.VMEM((2, rows_half, inner), f32)
    row8, row8_shape = whole_spec((8, features)), shape(8, features, f32)

    early_sum, late_sum = SeqSum(), SeqSum()

    def out_work(_):
        *kept["out"], keep, give = call(
            functools.partial(out_kernel, dims),
            (packs // half,),
            [chan_spec, model_spec, square],
            [piece_spec, piece_spec, send_spec] + half_specs,
            [piece_shape, piece_shape, shape(packs, 2, part, count, bf16)] + half_shapes,
            [Each((4, part, count), f32), half_sums],
            pre,
            gated, cot, w_out,
            us=6.8, group=half,
        )
        early_sum.put(keep, give)

    def z_work(_):
        keep, give, kept["gain"] = call(
            functools.partial(z_kernel, dims),
            (packs // half,),
            [model_spec, chan_spec, square],
            half_specs + [row8],
            half_shapes + [row8_shape],
            [half_sums],
            pre,
            normed, ggate, proj_z,
            us=5.3, group=half,
        )
        early_sum.put(keep, give)

    def diag_work(_):
        kept["diag"] = call(
            functools.partial(diag_kernel, dims),
            grid,
            [xbc_spec, lane_spec, chan_spec, chan_spec, state_spec, state_spec],
            [chan_spec, pack_spec((count, bc)), lane_spec],
            [
                shape(packs, count, inner, f32), shape(packs, count, bc, f32),
                shape(packs, count, LANES, f32),
            ],
            [],
            pre,
            xbc, steps, gy, y, state_keep, state_recv,
            us=12,
        )

    def early_work(_):
        early_sum.add(meta)
        own, far, send = kept["out"]
        own, far = call(
            out_gather_kernel, grid, [piece_spec, piece_spec, send_spec], [piece_spec, piece_spec],
            [piece_shape, shape(packs, part, count, bf16)], [], (), own, far, swap(send, "head", 1),
        )
        kept["out"] = own, swap(far, "head", 2)

    gstate_keep, gstate_recv = scan_states(
        gkeep, gsend, meta, packs, heads, size, 1, (out_work, z_work, diag_work, early_work),
        lambda: early_sum.got,
    )
    out_own, out_far = kept["out"]
    dx, dbc, sums = kept["diag"]

    edge_tile = (EDGE, inner)

    def pair_spec(shape_of):
        return pl.BlockSpec((half,) + shape_of, lambda p, *_: (p,) + (0,) * len(shape_of))

    pair_lane = pair_spec((count, LANES))
    share_own, share_near, grad_x, state_sums, edge_x = call(
        functools.partial(share_kernel, dims),
        (packs // half,),
        [xbc_spec, lane_spec, pack_spec((count, bc)), state_spec, state_spec, chan_spec, chan_spec,
         chan_spec, whole_spec((8, inner)), vec],
        [lane_spec, lane_spec, chan_spec, lane_spec, pack_spec(edge_tile)],
        [shape(packs, count, LANES, f32)] * 2
        + [shape(packs, count, inner, f32), shape(packs, count, LANES, f32),
           shape(packs, *edge_tile, bf16)],
        [Each((2 * EDGE, inner), f32)],
        pre,
        xbc, steps, dbc, gstate_keep, gstate_recv, gy, dx, slope_x, conv_own, skip,
        us=6.4, group=half,
    )
    share_near = swap(share_near, "head", 1)
    advance(early_sum, meta)
    two = shape(half, count, LANES, f32)
    bc_keep, bc_send = call(
        functools.partial(middle_kernel, (packs, bc_part)),
        (1,),
        [whole_spec((packs, count, LANES))] * 2,
        [whole_spec(two.shape)] * 2,
        [two, two],
        [],
        (meta,),
        share_own, share_near,
    )
    bc_recv = swap(bc_send, "head", 2)

    main_x, keep, give, grad_conv, gain_x = call(
        functools.partial(xback_kernel, dims),
        grid,
        [
            chan_spec, pack_spec((ext, inner)), model_spec, whole_spec((features, LANES)),
            pack_spec(edge_tile), whole_spec((8, inner)), square,
        ],
        [chan_spec, *half_specs, whole_spec((8, inner)), row8],
        [shape(packs, count, inner, bf16), *half_shapes, shape(8, inner, f32), row8_shape],
        [
            Each((count + EDGE, inner), f32), Each((ext, inner), f32), half_sums,
            pltpu.VMEM((LANES, inner), bf16),
        ],
        pre,
        grad_x, raw_x, normed, edge, edge_x, conv_own, proj_x,
        us=7, wait=(out_far,),
    )
    late_sum.put(keep, give)
    advance(early_sum, meta)

    gdt, gdt_rows, grad_small, gain_dt = call(
        functools.partial(step_kernel, dims),
        (packs // half,),
        [
            pair_lane, pair_lane, pair_lane, *[whole_spec((half,) + pay_shape)] * 4,
            whole_spec((8, LANES)), pair_spec((features, count)), whole_spec((features, LANES)),
        ],
        [pair_lane, row8, whole_spec((8, LANES)), row8],
        [shape(packs, count, LANES, bf16), row8_shape, shape(8, LANES, f32), row8_shape],
        [pltpu.VMEM((features, LANES), f32)],
        pre,
        steps, sums, state_sums, state_keep, state_recv, gstate_keep, gstate_recv, small, normed,
        w_dt,
        us=6,
    )
    advance(early_sum, meta)
    advance(late_sum, meta)
    give_rows = 2 * bc_part + 2 * SMALL
    gbc, edges, bc_sum, smalls = call(
        functools.partial(conv_bc_kernel, dims),
        grid,
        [
            half_spec((count, LANES), half), half_spec((count, LANES), half),
            pack_spec((count, bc_part)), pack_spec((ext, bc_part)), model_spec,
            whole_spec((features, LANES)), whole_spec((features, bc_part)),
            whole_spec((8, bc_part)), pack_spec(edge_tile), whole_spec((8, inner)), row8,
            whole_spec((8, LANES)), whole_spec((8, inner)), row8, row8, row8,
            whole_spec((features, 1)),
        ],
        [
            pack_spec((count, bc_part)), pack_spec((EDGE, inner + LANES)),
            whole_spec((give_rows, inner)), whole_spec((SMALL, inner)),
        ],
        [
            shape(packs, count, bc_part, bf16), shape(packs, EDGE, inner + LANES, bf16),
            shape(give_rows, inner, bf16), shape(SMALL, inner, f32),
        ],
        [
            Each((ext + EDGE, bc_part), f32), Each((ext, bc_part), f32),
            pltpu.VMEM((features, bc_part), f32), pltpu.VMEM((LANES, bc_part), bf16),
            pltpu.VMEM((8, bc_part), f32),
        ],
        pre,
        bc_keep, bc_recv, slope_bc, raw_bc, normed, edge, w_bc, conv_bc_own, edge_x, grad_conv,
        gdt_rows, grad_small, gate_small, kept["gain"], gain_x, gain_dt, gain_all,
        us=5,
    )
    edges = shift(edges, "seq", -1)
    bc_bits = [1 << k for k in range((lax.axis_size("seq") - 1).bit_length())]
    bc_got = swap(bc_sum, "seq", 1)
    advance(late_sum, meta)

    def bc_step(bit):
        nonlocal bc_sum, smalls, bc_got
        spec, small_spec = whole_spec(bc_sum.shape), whole_spec(smalls.shape)
        bc_sum, smalls = call(
            functools.partial(add_kernel, 1, False, [2 * bc_part], 1, True), (1,),
            [spec, spec, small_spec], [spec, small_spec],
            [shape(*bc_sum.shape, bf16), shape(*smalls.shape, f32)], [], (meta,),
            bc_sum, bc_got, smalls, us=0.01,
        )
        bc_got = swap(bc_sum, "seq", bit)

    bc_step(bc_bits[1])
    advance(early_sum, meta)

    tall = part + EDGE
    tall_send = pack_spec((2, tall, count))
    tall_spec = pack_spec((tall, count))
    row_spec, row_shape = pack_spec((1, count)), shape(packs, 1, count, f32)
    gn_own, gn_far, gn_send, dots = call(
        functools.partial(back_kernel, dims),
        (packs // half,),
        [
            chan_spec, pack_spec((EDGE, inner + LANES)), chan_spec, lane_spec,
            pack_spec((count, bc_part)), model_spec, square, square,
            whole_spec((features, bc_part)), whole_spec((features, LANES)),
        ],
        [piece_spec, piece_spec, tall_send, row_spec],
        [piece_shape, piece_shape, shape(packs, 2, tall, count, bf16), row_shape],
        [Each((4, part, count), f32)],
        pre,
        main_x, edges, ggate, gdt, gbc, normed, proj_z, proj_x, w_bc, w_dt,
        us=6, group=half,
    )
    near = swap(gn_send, "head", 1)
    order.drop(xbc, steps, normed)
    advance(late_sum, meta, 0.01, wait=(bc_got,))
    block_out = call(
        out_final_kernel, grid, [piece_spec] * 3, piece_spec, shape(packs, part, count, bf16), [],
        (), out_own, out_far, tokens, out=True, us=2,
    )
    block_out = jnp.swapaxes(block_out, 1, 2)

    gn_own, gn_far, dots = call(
        gather_kernel,
        grid,
        [piece_spec, piece_spec, tall_send, row_spec],
        [piece_spec, tall_spec, row_spec],
        [piece_shape, shape(packs, tall, count, bf16), row_shape],
        [],
        (),
        gn_own, gn_far, near, dots,
        us=0.01,
    )
    gn_far = swap(gn_far, "head", 2)
    order.hold(gn_own)
    while early_sum.bit != 0:
        advance(early_sum, meta)
    for bit in bc_bits[2:]:
        bc_step(bit)
    small_spec, give_spec = whole_spec(smalls.shape), whole_spec(bc_sum.shape)

    def head_step(x, bit):
        return call(
            plus_kernel, (1,), [small_spec, small_spec], small_spec, shape(*x.shape, f32), [], (),
            x, swap(x, "head", bit), us=0.01,
        )

    advance(late_sum, meta, 0.01)
    grads_out, grads_z = early_sum.result(meta, ("flip", "rows"), 2)
    while late_sum.bit != 0:
        advance(late_sum, meta, 0.01)
    grad_bc, smalls = call(
        functools.partial(whole_kernel, bc_part), (1,), [give_spec, give_spec, small_spec],
        [whole_spec((bc_part, features)), small_spec],
        [shape(bc_part, features, f32), shape(*smalls.shape, f32)], [], (), bc_sum, bc_got, smalls,
        us=0.01, out=1,
    )
    gains = head_step(smalls, 1)
    in_grad = call(
        functools.partial(final_kernel, (packs, count, features)),
        grid,
        [piece_spec, tall_spec, row_spec, piece_spec, row_spec, whole_spec((part, 1)), piece_spec],
        piece_spec,
        piece_shape,
        [],
        (),
        gn_own, gn_far, dots, tokens, inv, norm_gain_own, cotangent,
        us=2, out=True,
    )
    in_grad = jnp.swapaxes(in_grad, 1, 2)
    order.drop(gn_own)
    gains = head_step(gains, 2)
    vectors = [(inner,), (bc_part,), (heads,), (heads,), (heads,), (inner,), (part,)]
    tables = [(heads, features), (width, inner), (width, bc_part)]
    outs = call(
        functools.partial(unpack_kernel, (heads, features, bc_part, width)), (1,),
        [small_spec, small_spec], [whole_spec(x) for x in tables + vectors],
        [shape(*x, f32) for x in tables + vectors], [], (meta,), smalls, gains, out=True, us=0.01,
    )
    grad_dt, grad_conv, grad_conv_bc = outs[:3]
    bias_x_grad, bias_bc_grad, dt_bias_grad, a_log_grad, skip_grad, gate_grad, grad_gain = outs[3:]
    grads_x, = late_sum.result(meta, ("rows",))
    return (
        block_out,
        in_grad,
        grad_gain,
        grads_z,
        grads_x,
        grad_bc.T,
        grad_dt.T,
        grad_conv,
        grad_conv_bc,
        bias_x_grad,
        bias_bc_grad,
        dt_bias_grad,
        a_log_grad,
        skip_grad,
        gate_grad,
        grads_out,
    )


def solution(mesh):
    token, column, vector = P(None, "seq", "head"), P(None, "head"), P("head")
    row = P("head", None)
    return jax.shard_map(
        shards,
        mesh=mesh,
        in_specs=(
            token, token, P(), vector, column, column, column, column, column, column, vector,
            vector, vector, vector, vector, vector, row,
        ),
        out_specs=(
            token, token, vector, column, column, column, column, column, column, vector, vector,
            vector, vector, vector, vector, row,
        ),
        check_vma=False,
    )
```

profile of v0, /device:TPU:0, one launch (start us, length us, event | category | flops | bytes accessed | tf_op | source)
XLA Modules:
  0.0 194.3 jit_solution(18016172701778047314)
XLA Ops:
  0.8 3.0 %collective-permute-start.1 = (bf16[4,192,256]{2,1,0:T(8,128)(2,1)}, bf16[4,192,256]{2,1,0:T(8,128)(2,1)S(1)}, u32[]{:S(2)}, u32[]{:S(2)}) collective-permute-start(bf16[4,192,256]{2,1,0:T(8,128)(2,1)} %bitcast.10), channel_id=1, source_target_pairs={{0,2},{1,3},{2,0},{3,1},{4,6},{5,7},{6,4},{7,5},{8,10},{9,11},{10,... | collective-permute-start | bytes 1179656 | tf_op jit(solution)/shard_map/ppermute | solution.py:24
  5.5 3.4 %collective-permute-start.2 = (bf16[192,128]{1,0:T(8,128)(2,1)S(1)}, bf16[192,128]{1,0:T(8,128)(2,1)S(1)}, u32[]{:S(2)}, u32[]{:S(2)}) collective-permute-start(bf16[192,128]{1,0:T(8,128)(2,1)S(1)} %get-tuple-element.199), channel_id=1, source_target_pairs={{0,4},{4,8},{8,12},{12,16},{16,20},{20,24},{24,28},{1,5},{5,9},{9,... | collective-permute-start | bytes 147464 | tf_op jit(solution)/shard_map/ppermute | solution.py:24
  13.2 3.4 %collective-permute-done.3.refs_3_ = bf16[192,128]{1,0:T(8,128)(2,1)S(1)} collective-permute-done((bf16[192,128]{1,0:T(8,128)(2,1)S(1)}, bf16[192,128]{1,0:T(8,128)(2,1)S(1)}, u32[]{:S(2)}, u32[]{:S(2)}) %collective-permute-start.3) | collective-permute-done | bytes 49184 | tf_op jit(solution)/shard_map/ppermute | solution.py:24
  19.8 5.9 %shard_map.291 = (bf16[4,768,256]{2,1,0:T(8,128)(2,1)S(1)}, f32[4,1,256]{2,1,0:T(1,128)S(1)}, bf16[4,272,384]{2,1,0:T(8,128)(2,1)S(1)}, bf16[4,272,64]{2,1,0:T(8...) custom-call(s32[2]{0:T(128)S(1)} %pad_add_fusion.refs_0_, ...), custom_call_target="tpu_custom_call" | custom-call | flops 60000002048 | bytes 18000000 | tf_op jit(solution)/shard_map/pallas_call | solution.py:1157
  28.0 5.9 %shard_map.292 = (bf16[4,768,256]{2,1,0:T(8,128)(2,1)S(1)}, f32[4,1,256]{2,1,0:T(1,128)S(1)}, bf16[4,272,384]{2,1,0:T(8,128)(2,1)S(1)}, bf16[4,272,64]{2,1,0:T(8...) custom-call(s32[2]{0:T(128)S(1)} %pad_add_fusion.refs_0_, ...), custom_call_target="tpu_custom_call", output_to_operand_aliasing={{0}: (13, {}), {1}: (14, {}), {2}: (15, {}), {3}: (16, {}),... | custom-call | flops 60000002048 | bytes 18000000 | tf_op jit(solution)/shard_map/pallas_call | solution.py:1157
  38.0 4.1 %shard_map.294 = (bf16[4,256,384]{2,1,0:T(8,128)(2,1)S(1)}, f32[4,256,384]{2,1,0:T(8,128)S(1)}, f32[4,256,64]{2,1,0:T(8,128)S(1)}, f32[8,128]{1,0:T(8,128)S(1)}) custom-call(s32[2]{0:T(128)S(1)} %pad_add_fusion.refs_0_, s32[4,4]{1,0:T(4,128)S(1)} %copy-done.17, ...), custom_call_target="tpu_custom_call" | custom-call | flops 70000001024 | bytes 21000000 | tf_op jit(solution)/shard_map/pallas_call | solution.py:1157
  45.0 2.7 %collective-permute-start.12 = (s16[2,400,128]{2,1,0:T(8,128)(2,1)S(1)}, s16[2,400,128]{2,1,0:T(8,128)(2,1)S(1)}, u32[]{:S(2)}, u32[]{:S(2)}) collective-permute-start(s16[2,400,128]{2,1,0:T(8,128)(2,1)S(1)} %get-tuple-element.235), channel_id=1, source_target_pairs={{0,16},{4,20},{8,24},{12,28},{16,0},{20,4},{24,8},{28,12},{1,17},{... | collective-permute-start | bytes 614408 | tf_op jit(solution)/shard_map/ppermute | solution.py:24
  47.7 3.5 %shard_map.296 = (f32[4,256,384]{2,1,0:T(8,128)S(1)}, f32[8,128]{1,0:T(8,128)S(1)}) custom-call(s32[2]{0:T(128)S(1)} %pad_add_fusion.refs_0_, s32[4,4]{1,0:T(4,128)S(1)} %copy-done.17, bf16[4,256,640]{2,1,0:T(8,128)(2,1)S(1)} %get-tuple-element.221.refs_5_.refs_9_.refs_2_.refs_7_.refs_6_.refs_11_.refs_13_.refs_20_, ...), custom_call_target="tpu_custom_call" | custom-call | flops 60000002048 | bytes 18000000 | tf_op jit(solution)/shard_map/pallas_call | solution.py:1157
  51.2 6.0 %collective-permute-done.12.refs_3_ = s16[2,400,128]{2,1,0:T(8,128)(2,1)S(1)} collective-permute-done((s16[2,400,128]{2,1,0:T(8,128)(2,1)S(1)}, s16[2,400,128]{2,1,0:T(8,128)(2,1)S(1)}, u32[]{:S(2)}, u32[]{:S(2)}) %collective-permute-start.12) | collective-permute-done | bytes 204832 | tf_op jit(solution)/shard_map/ppermute | solution.py:24
  60.4 3.1 %shard_map.298 = (bf16[4,768,256]{2,1,0:T(8,128)(2,1)S(1)}, f32[4,256,384]{2,1,0:T(8,128)S(1)}, f32[8,128]{1,0:T(8,128)S(1)}) custom-call(s32[2]{0:T(128)S(1)} %pad_add_fusion.refs_0_, s32[4,4]{1,0:T(4,128)S(1)} %copy-done.17, bf16[4,192,256]{2,1,0:T(8,128)(2,1)} %bitcast.5.refs_2_.refs_6_, bf16[4,192,256]{2,1,0:T(8,128)(2,1)} %collective-permute-done.14.refs_3_, ...), custom_call_target="tpu_custom_call" | custom-call | flops 54999998464 | bytes 16500000 | tf_op jit(solution)/shard_map/pallas_call | solution.py:1157
  65.9 2.9 %shard_map.299 = (f32[4,256,384]{2,1,0:T(8,128)S(1)}, f32[4,2,256]{2,1,0:T(2,128)S(1)}, f32[8,128]{1,0:T(8,128)S(1)}) custom-call(s32[2]{0:T(128)S(1)} %pad_add_fusion.refs_0_, s32[4,4]{1,0:T(4,128)S(1)} %copy-done.17, bf16[4,256,640]{2,1,0:T(8,128)(2,1)S(1)} %get-tuple-element.221.refs_5_.refs_9_.refs_2_.refs_7_.refs_6_.refs_11_.refs_13_.refs_20_, ...), custom_call_target="tpu_custom_call" | custom-call | flops 65999998976 | bytes 19800000 | tf_op jit(solution)/shard_map/pallas_call | solution.py:1157
  69.9 2.6 %collective-permute-done.18.refs_4_ = f32[4,2,256]{2,1,0:T(2,128)S(1)} collective-permute-done((f32[4,2,256]{2,1,0:T(2,128)S(1)}, f32[4,2,256]{2,1,0:T(2,128)S(1)}, u32[]{:S(2)}, u32[]{:S(2)}) %collective-permute-start.18) | collective-permute-done | bytes 8224 | tf_op jit(solution)/shard_map/ppermute | solution.py:24
  73.7 5.7 %shard_map.300 = (f32[4,256,384]{2,1,0:T(8,128)S(1)}, bf16[4,256,384]{2,1,0:T(8,128)(2,1)S(1)}, bf16[4,256,384]{2,1,0:T(8,128)(2,1)S(1)}, s16[2,400,128]{2,1,0:T...) custom-call(s32[2]{0:T(128)S(1)} %pad_add_fusion.refs_0_, ...), custom_call_target="tpu_custom_call" | custom-call | flops 83000000512 | bytes 24900000 | tf_op jit(solution)/shard_map/pallas_call | solution.py:1157
  80.8 4.0 %shard_map.301 = (f32[4,192,256]{2,1,0:T(8,128)S(1)}, f32[4,192,256]{2,1,0:T(8,128)S(1)}, bf16[4,2,192,256]{3,2,1,0:T(8,128)(2,1)}, f32[384,384]{1,0:T(8,128)S(1...) custom-call(s32[2]{0:T(128)S(1)} %pad_add_fusion.refs_0_, s32[4,4]{1,0:T(4,128)S(1)} %copy-done.17, ...), custom_call_target="tpu_custom_call" | custom-call | flops 67999997952 | bytes 20400000 | tf_op jit(solution)/shard_map/pallas_call | solution.py:1157
  97.5 7.4 %shard_map.305 = (f32[4,256,384]{2,1,0:T(8,128)S(1)}, f32[4,256,256]{2,1,0:T(8,128)S(1)}, f32[4,256,128]{2,1,0:T(8,128)S(1)}, f32[8,128]{1,0:T(8,128)S(1)}) custom-call(s32[2]{0:T(128)S(1)} %pad_add_fusion.refs_0_, s32[4,4]{1,0:T(4,128)S(1)} %copy-done.17, ...), custom_call_target="tpu_custom_call" | custom-call | flops 120000004096 | bytes 36000000 | tf_op jit(solution)/shard_map/pallas_call | solution.py:1157
  114.3 4.0 %shard_map.309 = (f32[4,256,128]{2,1,0:T(8,128)S(1)}, f32[4,256,128]{2,1,0:T(8,128)S(1)}, f32[4,256,384]{2,1,0:T(8,128)S(1)}, f32[4,256,128]{2,1,0:T(8,128)S(1)}...) custom-call(s32[2]{0:T(128)S(1)} %pad_add_fusion.refs_0_, s32[4,4]{1,0:T(4,128)S(1)} %copy-done.17, ...), custom_call_target="tpu_custom_call" | custom-call | flops 64000000000 | bytes 19200000 | tf_op jit(solution)/shard_map/pallas_call | solution.py:1157
  119.1 3.4 %collective-permute-start.31 = (bf16[192,384]{1,0:T(8,128)(2,1)S(1)}, bf16[192,384]{1,0:T(8,128)(2,1)S(1)}, u32[]{:S(2)}, u32[]{:S(2)}) collective-permute-start(bf16[192,384]{1,0:T(8,128)(2,1)S(1)} %get-tuple-element.297), channel_id=1, source_target_pairs={{0,16},{4,20},{8,24},{12,28},{16,0},{20,4},{24,8},{28,12},{1,17},{... | collective-permute-start | bytes 442376 | tf_op jit(solution)/shard_map/ppermute | solution.py:24
  123.8 5.4 %shard_map.312 = (bf16[4,256,384]{2,1,0:T(8,128)(2,1)S(1)}, f32[384,384]{1,0:T(8,128)S(1)}, bf16[384,384]{1,0:T(8,128)(2,1)S(1)}, f32[8,384]{1,0:T(8,128)S(1)}, ...) custom-call(s32[2]{0:T(128)S(1)} %pad_add_fusion.refs_0_, s32[4,4]{1,0:T(4,128)S(1)} %copy-done.17, ...), custom_call_target="tpu_custom_call" | custom-call | flops 70000001024 | bytes 21000000 | tf_op jit(solution)/shard_map/pallas_call | solution.py:1157
  134.8 4.4 %shard_map.314 = (bf16[4,256,128]{2,1,0:T(8,128)(2,1)S(1)}, f32[8,768]{1,0:T(8,128)S(1)}, f32[8,128]{1,0:T(8,128)S(1)}, f32[8,768]{1,0:T(8,128)S(1)}, f32[8,128]{1,0:T(8,128)S(1)}) custom-call(s32[2]{0:T(128)S(1)} %pad_add_fusion.refs_0_, s32[4,4]{1,0:T(4,128)S(1)} %copy-done.17, ...), custom_call_target="tpu_custom_call" | custom-call | flops 60000002048 | bytes 18000000 | tf_op jit(solution)/shard_map/pallas_call | solution.py:1157
  143.9 4.2 %shard_map.317 = (bf16[4,256,64]{2,1,0:T(8,128)(2,1)S(1)}, bf16[4,16,512]{2,1,0:T(8,128)(2,1)S(1)}, bf16[192,384]{1,0:T(8,128)(2,1)S(1)}, f32[32,384]{1,0:T(8,128)S(1)}, f32[8,128]{1,0:T(8,128)S(1)}) custom-call(s32[2]{0:T(128)S(1)} %pad_add_fusion.refs_0_, s32[4,4]{1,0:T(4,128)S(1)} %copy-done.17, f32[2,256,128]{2,1,0:T(8,128)S(1)} %get-tuple-element.308.refs_2_, ...), custom_call_target="tpu_custom_call" | custom-call | flops 49999998976 | bytes 15000000 | tf_op jit(solution)/shard_map/pallas_call | solution.py:1157
  149.4 2.7 %collective-permute-start.38 = (bf16[192,384]{1,0:T(8,128)(2,1)S(1)}, bf16[192,384]{1,0:T(8,128)(2,1)S(1)}, u32[]{:S(2)}, u32[]{:S(2)}) collective-permute-start(bf16[192,384]{1,0:T(8,128)(2,1)S(1)} %get-tuple-element.328.refs_1_), channel_id=1, source_target_pairs={{0,4},{4,0},{8,12},{12,8},{16,20},{20,16},{24,28},{28,24},{1,5},{5... | collective-permute-start | bytes 442376 | tf_op jit(solution)/shard_map/ppermute | solution.py:24
  160.5 3.7 %shard_map.321 = (f32[4,192,256]{2,1,0:T(8,128)S(1)}, f32[4,192,256]{2,1,0:T(8,128)S(1)}, bf16[4,2,208,256]{3,2,1,0:T(8,128)(2,1)S(1)}, f32[4,1,256]{2,1,0:T(1,128)S(1)}, f32[8,128]{1,0:T(8,128)S(1)}) custom-call(s32[2]{0:T(128)S(1)} %pad_add_fusion.refs_0_, s32[4,4]{1,0:T(4,128)S(1)} %copy-done.17, bf16[4,256,384]{2,1,0:T(8,128)(2,1)S(1)} %get-tuple-element.323.refs_2_, ...), custom_call_target="tpu_custom_call" | custom-call | flops 60000002048 | bytes 18000000 | tf_op jit(solution)/shard_map/pallas_call | solution.py:1157
  167.9 4.3 %collective-permute-done.43.refs_2_ = bf16[96,384]{1,0:T(8,128)(2,1)S(1)} collective-permute-done((bf16[96,384]{1,0:T(8,128)(2,1)S(1)}, bf16[96,384]{1,0:T(8,128)(2,1)S(1)}, u32[]{:S(2)}, u32[]{:S(2)}) %collective-permute-start.43) | collective-permute-done | bytes 73760 | tf_op jit(solution)/shard_map/ppermute | solution.py:24
  185.7 3.4 %shard_map.331 = (f32[4,192,256]{2,1,0:T(8,128)}, f32[8,128]{1,0:T(8,128)S(1)}) custom-call(f32[4,192,256]{2,1,0:T(8,128)S(1)} %get-tuple-element.342.refs_5_.refs_4_.refs_3_.refs_0_, bf16[4,208,256]{2,1,0:T(8,128)(2,1)S(1)} %collective-permute-done.41.refs_1_, f32[4,1,256]{2,1,0:T(1,128)S(1)} %get-tuple-element.344.refs_2_, ...), custom_call_target="tpu_custom_call" | custom-call | flops 20000000000 | bytes 6000000 | tf_op jit(solution)/shard_map/pallas_call | solution.py:1157
  (212 shorter events, 93.9 us)
Async XLA Ops:
  0.8 15.9 %collective-permute-start.1 = (bf16[4,192,256]{2,1,0:T(8,128)(2,1)}, bf16[4,192,256]{2,1,0:T(8,128)(2,1)S(1)}, u32[]{:S(2)}, u32[]{:S(2)}) collective-permute-start(bf16[4,192,256]{2,1,0:T(8,128)(2,1)} %bitcast.10), channel_id=1, source_target_pairs={{0,2},{1,3},{2,0},{3,1},{4,6},{5,7},{6,4},{7,5},{8,10},{9,11},{10,... | collective-permute-start | bytes 1179656 | tf_op jit(solution)/shard_map/ppermute | solution.py:24
  25.6 9.8 %collective-permute-start.10 = (s16[2,400,128]{2,1,0:T(8,128)(2,1)S(1)}, s16[2,400,128]{2,1,0:T(8,128)(2,1)S(1)}, u32[]{:S(2)}, u32[]{:S(2)}) collective-permute-start(s16[2,400,128]{2,1,0:T(8,128)(2,1)S(1)} %get-tuple-element.224), channel_id=1, source_target_pairs={{0,4},{4,0},{8,12},{12,8},{16,20},{20,16},{24,28},{28,24},{1,5},{5... | collective-permute-start | bytes 614408 | tf_op jit(solution)/shard_map/ppermute | solution.py:24
  34.5 23.9 %collective-permute-start.15 = (bf16[4,192,256]{2,1,0:T(8,128)(2,1)}, bf16[4,192,256]{2,1,0:T(8,128)(2,1)}, u32[]{:S(2)}, u32[]{:S(2)}) collective-permute-start(bf16[4,192,256]{2,1,0:T(8,128)(2,1)} %bitcast.5.refs_2_.refs_6_), channel_id=1, source_target_pairs={{0,2},{1,3},{2,0},{3,1},{4,6},{5,7},{6,4},{7,5},{8,10},{9,11},{10,... | collective-permute-start | bytes 1179656 | tf_op jit(solution)/shard_map/ppermute | solution.py:24
  35.4 24.3 %collective-permute-start.14 = (bf16[4,192,256]{2,1,0:T(8,128)(2,1)}, bf16[4,192,256]{2,1,0:T(8,128)(2,1)}, u32[]{:S(2)}, u32[]{:S(2)}) collective-permute-start(bf16[4,192,256]{2,1,0:T(8,128)(2,1)} %bitcast.5.refs_2_.refs_6_), channel_id=1, source_target_pairs={{0,1},{1,0},{2,3},{3,2},{4,5},{5,4},{6,7},{7,6},{8,9},{9,8},{10,11... | collective-permute-start | bytes 1179656 | tf_op jit(solution)/shard_map/ppermute | solution.py:24
  36.4 7.5 %collective-permute-start.11 = (s16[2,400,128]{2,1,0:T(8,128)(2,1)S(1)}, s16[2,400,128]{2,1,0:T(8,128)(2,1)S(1)}, u32[]{:S(2)}, u32[]{:S(2)}) collective-permute-start(s16[2,400,128]{2,1,0:T(8,128)(2,1)S(1)} %get-tuple-element.227.refs_1_), channel_id=1, source_target_pairs={{0,8},{4,12},{8,0},{12,4},{16,24},{20,28},{24,16},{28,20},{1,9},{5... | collective-permute-start | bytes 614408 | tf_op jit(solution)/shard_map/ppermute | solution.py:24
  45.0 12.2 %collective-permute-start.12 = (s16[2,400,128]{2,1,0:T(8,128)(2,1)S(1)}, s16[2,400,128]{2,1,0:T(8,128)(2,1)S(1)}, u32[]{:S(2)}, u32[]{:S(2)}) collective-permute-start(s16[2,400,128]{2,1,0:T(8,128)(2,1)S(1)} %get-tuple-element.235), channel_id=1, source_target_pairs={{0,16},{4,20},{8,24},{12,28},{16,0},{20,4},{24,8},{28,12},{1,17},{... | collective-permute-start | bytes 614408 | tf_op jit(solution)/shard_map/ppermute | solution.py:24
  84.8 20.2 %collective-permute-start.22 = (bf16[384,384]{1,0:T(8,128)(2,1)}, bf16[384,384]{1,0:T(8,128)(2,1)}, u32[]{:S(2)}, u32[]{:S(2)}) collective-permute-start(bf16[384,384]{1,0:T(8,128)(2,1)} %get-tuple-element.265), channel_id=1, source_target_pairs={{0,4},{4,0},{8,12},{12,8},{16,20},{20,16},{24,28},{28,24},{1,5},{5... | collective-permute-start | bytes 884744 | tf_op jit(solution)/shard_map/ppermute | solution.py:24
  85.6 25.4 %collective-permute-start.20 = (bf16[4,2,192,256]{3,2,1,0:T(8,128)(2,1)}, bf16[4,2,192,256]{3,2,1,0:T(8,128)(2,1)}, u32[]{:S(2)}, u32[]{:S(2)}) collective-permute-start(bf16[4,2,192,256]{3,2,1,0:T(8,128)(2,1)} %get-tuple-element.257), channel_id=1, source_target_pairs={{0,1},{1,0},{2,3},{3,2},{4,5},{5,4},{6,7},{7,6},{8,9},{9,8},{10,11... | collective-permute-start | bytes 2359304 | tf_op jit(solution)/shard_map/ppermute | solution.py:24
  90.5 14.5 %collective-permute-start.23 = (bf16[384,384]{1,0:T(8,128)(2,1)S(1)}, bf16[384,384]{1,0:T(8,128)(2,1)S(1)}, u32[]{:S(2)}, u32[]{:S(2)}) collective-permute-start(bf16[384,384]{1,0:T(8,128)(2,1)S(1)} %get-tuple-element.266), channel_id=1, source_target_pairs={{0,4},{4,0},{8,12},{12,8},{16,20},{20,16},{24,28},{28,24},{1,5},{5... | collective-permute-start | bytes 884744 | tf_op jit(solution)/shard_map/ppermute | solution.py:24
  95.1 10.9 %collective-permute-start.25 = (s16[2,400,128]{2,1,0:T(8,128)(2,1)S(1)}, s16[2,400,128]{2,1,0:T(8,128)(2,1)S(1)}, u32[]{:S(2)}, u32[]{:S(2)}) collective-permute-start(s16[2,400,128]{2,1,0:T(8,128)(2,1)S(1)} %get-tuple-element.269), channel_id=1, source_target_pairs={{0,16},{4,20},{8,24},{12,28},{16,0},{20,4},{24,8},{28,12},{1,17},{... | collective-permute-start | bytes 614408 | tf_op jit(solution)/shard_map/ppermute | solution.py:24
  110.2 8.3 %collective-permute-start.29 = (bf16[384,384]{1,0:T(8,128)(2,1)S(1)}, bf16[384,384]{1,0:T(8,128)(2,1)S(1)}, u32[]{:S(2)}, u32[]{:S(2)}) collective-permute-start(bf16[384,384]{1,0:T(8,128)(2,1)S(1)} %get-tuple-element.290), channel_id=1, source_target_pairs={{0,8},{4,12},{8,0},{12,4},{16,24},{20,28},{24,16},{28,20},{1,9},{5... | collective-permute-start | bytes 884744 | tf_op jit(solution)/shard_map/ppermute | solution.py:24
  113.0 10.4 %collective-permute-start.26 = (bf16[4,192,256]{2,1,0:T(8,128)(2,1)S(1)}, bf16[4,192,256]{2,1,0:T(8,128)(2,1)S(1)}, u32[]{:S(2)}, u32[]{:S(2)}) collective-permute-start(bf16[4,192,256]{2,1,0:T(8,128)(2,1)S(1)} %get-tuple-element.277), channel_id=1, source_target_pairs={{0,2},{1,3},{2,0},{3,1},{4,6},{5,7},{6,4},{7,5},{8,10},{9,11},{10,... | collective-permute-start | bytes 1179656 | tf_op jit(solution)/shard_map/ppermute | solution.py:24
  119.1 11.0 %collective-permute-start.31 = (bf16[192,384]{1,0:T(8,128)(2,1)S(1)}, bf16[192,384]{1,0:T(8,128)(2,1)S(1)}, u32[]{:S(2)}, u32[]{:S(2)}) collective-permute-start(bf16[192,384]{1,0:T(8,128)(2,1)S(1)} %get-tuple-element.297), channel_id=1, source_target_pairs={{0,16},{4,20},{8,24},{12,28},{16,0},{20,4},{24,8},{28,12},{1,17},{... | collective-permute-start | bytes 442376 | tf_op jit(solution)/shard_map/ppermute | solution.py:24
  130.7 9.4 %collective-permute-start.32 = (bf16[192,384]{1,0:T(8,128)(2,1)S(1)}, bf16[192,384]{1,0:T(8,128)(2,1)S(1)}, u32[]{:S(2)}, u32[]{:S(2)}) collective-permute-start(bf16[192,384]{1,0:T(8,128)(2,1)S(1)} %get-tuple-element.299.refs_1_), channel_id=1, source_target_pairs={{0,16},{4,20},{8,24},{12,28},{16,0},{20,4},{24,8},{28,12},{1,17},{... | collective-permute-start | bytes 442376 | tf_op jit(solution)/shard_map/ppermute | solution.py:24
  133.0 10.9 %collective-permute-start.34 = (f32[2,256,128]{2,1,0:T(8,128)S(1)}, f32[2,256,128]{2,1,0:T(8,128)S(1)}, u32[]{:S(2)}, u32[]{:S(2)}) collective-permute-start(f32[2,256,128]{2,1,0:T(8,128)S(1)} %get-tuple-element.309), channel_id=1, source_target_pairs={{0,2},{1,3},{2,0},{3,1},{4,6},{5,7},{6,4},{7,5},{8,10},{9,11},{10,... | collective-permute-start | bytes 786440 | tf_op jit(solution)/shard_map/ppermute | solution.py:24
  140.7 18.4 %collective-permute-start.37 = (bf16[384,384]{1,0:T(8,128)(2,1)S(1)}, bf16[384,384]{1,0:T(8,128)(2,1)S(1)}, u32[]{:S(2)}, u32[]{:S(2)}) collective-permute-start(bf16[384,384]{1,0:T(8,128)(2,1)S(1)} %get-tuple-element.327.refs_1_), channel_id=1, source_target_pairs={{0,8},{4,12},{8,0},{12,4},{16,24},{20,28},{24,16},{28,20},{1,9},{5... | collective-permute-start | bytes 884744 | tf_op jit(solution)/shard_map/ppermute | solution.py:24
  142.3 11.3 %collective-permute-start.33 = (bf16[192,384]{1,0:T(8,128)(2,1)S(1)}, bf16[192,384]{1,0:T(8,128)(2,1)S(1)}, u32[]{:S(2)}, u32[]{:S(2)}) collective-permute-start(bf16[192,384]{1,0:T(8,128)(2,1)S(1)} %get-tuple-element.307), channel_id=1, source_target_pairs={{0,8},{4,12},{8,0},{12,4},{16,24},{20,28},{24,16},{28,20},{1,9},{5... | collective-permute-start | bytes 442376 | tf_op jit(solution)/shard_map/ppermute | solution.py:24
  148.1 12.2 %collective-permute-start.36 = (bf16[4,16,512]{2,1,0:T(8,128)(2,1)S(1)}, bf16[4,16,512]{2,1,0:T(8,128)(2,1)S(1)}, u32[]{:S(2)}, u32[]{:S(2)}) collective-permute-start(bf16[4,16,512]{2,1,0:T(8,128)(2,1)S(1)} %get-tuple-element.324), channel_id=1, source_target_pairs={{4,0},{8,4},{12,8},{16,12},{20,16},{24,20},{28,24},{5,1},{9,5},{13... | collective-permute-start | bytes 196616 | tf_op jit(solution)/shard_map/ppermute | solution.py:24
  154.1 10.2 %collective-permute-start.35 = (bf16[96,384]{1,0:T(8,128)(2,1)S(1)}, bf16[96,384]{1,0:T(8,128)(2,1)S(1)}, u32[]{:S(2)}, u32[]{:S(2)}) collective-permute-start(bf16[96,384]{1,0:T(8,128)(2,1)S(1)} %get-tuple-element.322), channel_id=1, source_target_pairs={{0,16},{4,20},{8,24},{12,28},{16,0},{20,4},{24,8},{28,12},{1,17},{... | collective-permute-start | bytes 221192 | tf_op jit(solution)/shard_map/ppermute | solution.py:24
  156.8 7.6 %collective-permute-start.39 = (bf16[192,384]{1,0:T(8,128)(2,1)S(1)}, bf16[192,384]{1,0:T(8,128)(2,1)S(1)}, u32[]{:S(2)}, u32[]{:S(2)}) collective-permute-start(bf16[192,384]{1,0:T(8,128)(2,1)S(1)} %get-tuple-element.334.refs_1_), channel_id=1, source_target_pairs={{0,8},{4,12},{8,0},{12,4},{16,24},{20,28},{24,16},{28,20},{1,9},{5... | collective-permute-start | bytes 442376 | tf_op jit(solution)/shard_map/ppermute | solution.py:24
  159.8 16.3 %collective-permute-start.45 = (bf16[768,384]{1,0:T(8,128)(2,1)S(1)}, bf16[768,384]{1,0:T(8,128)(2,1)S(1)}, u32[]{:S(2)}, u32[]{:S(2)}) collective-permute-start(bf16[768,384]{1,0:T(8,128)(2,1)S(1)} %get-tuple-element.354.refs_1_), channel_id=1, source_target_pairs={{0,4},{4,0},{8,12},{12,8},{16,20},{20,16},{24,28},{28,24},{1,5},{5... | collective-permute-start | bytes 1769480 | tf_op jit(solution)/shard_map/ppermute | solution.py:24
  172.8 9.6 %collective-permute-start.42 = (bf16[192,384]{1,0:T(8,128)(2,1)S(1)}, bf16[192,384]{1,0:T(8,128)(2,1)S(1)}, u32[]{:S(2)}, u32[]{:S(2)}) collective-permute-start(bf16[192,384]{1,0:T(8,128)(2,1)S(1)} %get-tuple-element.349.refs_0_), channel_id=1, source_target_pairs={{0,16},{4,20},{8,24},{12,28},{16,0},{20,4},{24,8},{28,12},{1,17},{... | collective-permute-start | bytes 442376 | tf_op jit(solution)/shard_map/ppermute | solution.py:24
  174.6 11.0 %collective-permute-start.41 = (bf16[4,208,256]{2,1,0:T(8,128)(2,1)S(1)}, bf16[4,208,256]{2,1,0:T(8,128)(2,1)S(1)}, u32[]{:S(2)}, u32[]{:S(2)}) collective-permute-start(bf16[4,208,256]{2,1,0:T(8,128)(2,1)S(1)} %get-tuple-element.343), channel_id=1, source_target_pairs={{0,2},{1,3},{2,0},{3,1},{4,6},{5,7},{6,4},{7,5},{8,10},{9,11},{10,... | collective-permute-start | bytes 1277960 | tf_op jit(solution)/shard_map/ppermute | solution.py:24
  183.1 9.4 %collective-permute-start.48 = (bf16[384,384]{1,0:T(8,128)(2,1)S(1)}, bf16[384,384]{1,0:T(8,128)(2,1)S(1)}, u32[]{:S(2)}, u32[]{:S(2)}) collective-permute-start(bf16[384,384]{1,0:T(8,128)(2,1)S(1)} %get-tuple-element.368.refs_1_), channel_id=1, source_target_pairs={{0,4},{4,0},{8,12},{12,8},{16,20},{20,16},{24,28},{28,24},{1,5},{5... | collective-permute-start | bytes 884744 | tf_op jit(solution)/shard_map/ppermute | solution.py:24
  (70 other events, 413.6 us)
where the time goes:
time: 195 us; the launch traced here: 194 us
  Pallas kernels  98 us (50%)
  starting transfers between devices  53.5 us (27%)
  waiting for transfers between devices  40 us (21%)
    pallas_call x47, Pallas kernels, call(): pl.pallas_call(body, grid_spec=pltpu.PrefetchScalarGridSpec(num_scalar_pr...  98 us
    ppermute x49, starting transfers between devices, permuted(): y = lax.ppermute(x, axis, route)  53.5 us
    ppermute x49, waiting for transfers between devices, permuted(): y = lax.ppermute(x, axis, route)  40 us
  transfers between devices with their start and end apart: 49, of which 23 were waited for; matrix products, arithmetic and copies ran while one was open for 0% of the time, Pallas kernels for 42%

commit v1 on v0

--- a/solution.py
+++ b/solution.py
@@ -983,6 +983,10 @@
         read += rows
 
 
+def part_kernel(values, out):
+    out[0] = values[...].astype(f32)
+
+
 def result_kernel(segs, ways, meta, mine, got, *outs):
     first = (meta[0] & 1) == 0
     read = 0
@@ -1281,6 +1285,19 @@
         )]
         self.segs = [2 * rows for rows in self.segs]
 
+    def half_result(self, meta, mine, onto=()):
+        rows, cols = self.keep[0].shape
+
+        def index(p, pre, grouped):
+            side = pre[0][0] & 1
+            return side if mine else 1 - side
+
+        return call(
+            lambda meta, values, out: part_kernel(values, out), (1,), [whole_spec((rows, cols))],
+            Spec((rows, cols), index), shape(2, rows, cols, f32), [], (meta,),
+            self.keep[0] if mine else self.got[0], out=True, us=0.01, onto=onto,
+        )
+
     def result(self, meta, ways, us=0.01):
         cols = self.keep[0].shape[1]
         shapes = {"rows": lambda r: (2 * r, cols), "flip": lambda r: (cols, 2 * r), "cols": lambda r: (r, 2 * cols)}
@@ -1497,7 +1514,7 @@
         xbc, steps, inner_out, state_keep, state_recv, gate, gg, gain_gate, skip,
         us=6.6, group=half,
     )
-    stats = head_pieces(stats)
+    stats = [stats] + [swap(stats, "head", bits) for bits in (1, 2, 3)]
 
     gy, gated, ggate, gkeep, gsend, gate_small = call(
         functools.partial(grad_kernel, dims, total_inner),
@@ -1552,6 +1569,12 @@
             us=5.3, group=half,
         )
         early_sum.put(keep, give)
+        own, far, send = kept["out"]
+        own, far = call(
+            out_gather_kernel, grid, [piece_spec, piece_spec, send_spec], [piece_spec, piece_spec],
+            [piece_shape, shape(packs, part, count, bf16)], [], (), own, far, swap(send, "head", 1),
+        )
+        kept["out"] = own, swap(far, "head", 2)
 
     def diag_work(_):
         kept["diag"] = call(
@@ -1571,12 +1594,6 @@
 
     def early_work(_):
         early_sum.add(meta)
-        own, far, send = kept["out"]
-        own, far = call(
-            out_gather_kernel, grid, [piece_spec, piece_spec, send_spec], [piece_spec, piece_spec],
-            [piece_shape, shape(packs, part, count, bf16)], [], (), own, far, swap(send, "head", 1),
-        )
-        kept["out"] = own, swap(far, "head", 2)
 
     gstate_keep, gstate_recv = scan_states(
         gkeep, gsend, meta, packs, heads, size, 1, (out_work, z_work, diag_work, early_work),
@@ -1729,8 +1746,8 @@
     order.drop(xbc, steps, normed)
     advance(late_sum, meta, 0.01, wait=(bc_got,))
     block_out = call(
-        out_final_kernel, grid, [piece_spec] * 3, piece_spec, shape(packs, part, count, bf16), [],
-        (), out_own, out_far, tokens, out=True, us=2,
+        out_final_kernel, (packs // half,), [piece_spec] * 3, piece_spec, shape(packs, part, count, bf16), [],
+        (), out_own, out_far, tokens, out=True, us=2, group=half,
     )
     block_out = jnp.swapaxes(block_out, 1, 2)
 
@@ -1760,7 +1777,7 @@
         )
 
     advance(late_sum, meta, 0.01)
-    grads_out, grads_z = early_sum.result(meta, ("flip", "rows"), 2)
+    grads_out, grads_z = early_sum.result(meta, ("flip", "rows"), 0.4)
     while late_sum.bit != 0:
         advance(late_sum, meta, 0.01)
     grad_bc, smalls = call(
@@ -1772,18 +1789,19 @@
     gains = head_step(smalls, 1)
     in_grad = call(
         functools.partial(final_kernel, (packs, count, features)),
-        grid,
+        (packs // half,),
         [piece_spec, tall_spec, row_spec, piece_spec, row_spec, whole_spec((part, 1)), piece_spec],
         piece_spec,
         piece_shape,
         [],
         (),
         gn_own, gn_far, dots, tokens, inv, norm_gain_own, cotangent,
-        us=2, out=True,
+        us=2, out=True, group=half,
     )
     in_grad = jnp.swapaxes(in_grad, 1, 2)
     order.drop(gn_own)
     gains = head_step(gains, 2)
+    own_half = late_sum.half_result(meta, True)
     vectors = [(inner,), (bc_part,), (heads,), (heads,), (heads,), (inner,), (part,)]
     tables = [(heads, features), (width, inner), (width, bc_part)]
     outs = call(
@@ -1793,7 +1811,7 @@
     )
     grad_dt, grad_conv, grad_conv_bc = outs[:3]
     bias_x_grad, bias_bc_grad, dt_bias_grad, a_log_grad, skip_grad, gate_grad, grad_gain = outs[3:]
-    grads_x, = late_sum.result(meta, ("rows",))
+    grads_x = late_sum.half_result(meta, False, (own_half,)).reshape(features, inner)
     return (
         block_out,
         in_grad,

time: 195 us -> 192 us (0.985)
  waiting for transfers between devices: 40 us -> 36.2 us
    ppermute x49, waiting for transfers between devices: 40 us -> 36.2 us  [permuted(): y = lax.ppermute(x, axis, route)]
    pallas_call x47 -> x48, Pallas kernels: 98 us -> 97.2 us  [call(): pl.pallas_call(body, grid_spec=pltpu.PrefetchScalarGridSpec(num_scalar_pr...]
where the time goes in v1:
time: 192 us; the launch traced here: 191 us
  Pallas kernels  97.2 us (51%)
  starting transfers between devices  55 us (29%)
  waiting for transfers between devices  36.2 us (19%)
    pallas_call x48, Pallas kernels, call(): pl.pallas_call(body, grid_spec=pltpu.PrefetchScalarGridSpec(num_scalar_pr...  97.2 us
    ppermute x49, starting transfers between devices, permuted(): y = lax.ppermute(x, axis, route)  55 us
    ppermute x49, waiting for transfers between devices, permuted(): y = lax.ppermute(x, axis, route)  36.2 us
  transfers between devices with their start and end apart: 49, of which 23 were waited for; matrix products, arithmetic and copies ran while one was open for 0% of the time, Pallas kernels for 42%

profile of v1, /device:TPU:0, one launch (start us, length us, event | category | flops | bytes accessed | tf_op | source)
XLA Modules:
  0.0 191.4 jit_solution(16245356742535987528)
XLA Ops:
  0.8 3.0 %collective-permute-start.1 = (bf16[4,192,256]{2,1,0:T(8,128)(2,1)}, bf16[4,192,256]{2,1,0:T(8,128)(2,1)S(1)}, u32[]{:S(2)}, u32[]{:S(2)}) collective-permute-start(bf16[4,192,256]{2,1,0:T(8,128)(2,1)} %bitcast.11), channel_id=1, source_target_pairs={{0,2},{1,3},{2,0},{3,1},{4,6},{5,7},{6,4},{7,5},{8,10},{9,11},{10,... | collective-permute-start | bytes 1179656 | tf_op jit(solution)/shard_map/ppermute | solution.py:24
  5.5 3.4 %collective-permute-start.2 = (bf16[192,128]{1,0:T(8,128)(2,1)S(1)}, bf16[192,128]{1,0:T(8,128)(2,1)S(1)}, u32[]{:S(2)}, u32[]{:S(2)}) collective-permute-start(bf16[192,128]{1,0:T(8,128)(2,1)S(1)} %get-tuple-element.201), channel_id=1, source_target_pairs={{0,4},{4,8},{8,12},{12,16},{16,20},{20,24},{24,28},{1,5},{5,9},{9,... | collective-permute-start | bytes 147464 | tf_op jit(solution)/shard_map/ppermute | solution.py:24
  13.2 3.4 %collective-permute-done.3.refs_3_ = bf16[192,128]{1,0:T(8,128)(2,1)S(1)} collective-permute-done((bf16[192,128]{1,0:T(8,128)(2,1)S(1)}, bf16[192,128]{1,0:T(8,128)(2,1)S(1)}, u32[]{:S(2)}, u32[]{:S(2)}) %collective-permute-start.3) | collective-permute-done | bytes 49184 | tf_op jit(solution)/shard_map/ppermute | solution.py:24
  19.8 5.9 %shard_map.291 = (bf16[4,768,256]{2,1,0:T(8,128)(2,1)S(1)}, f32[4,1,256]{2,1,0:T(1,128)S(1)}, bf16[4,272,384]{2,1,0:T(8,128)(2,1)S(1)}, bf16[4,272,64]{2,1,0:T(8...) custom-call(s32[2]{0:T(128)S(1)} %pad_add_fusion.refs_0_, ...), custom_call_target="tpu_custom_call" | custom-call | flops 60000002048 | bytes 18000000 | tf_op jit(solution)/shard_map/pallas_call | solution.py:1161
  28.0 5.9 %shard_map.292 = (bf16[4,768,256]{2,1,0:T(8,128)(2,1)S(1)}, f32[4,1,256]{2,1,0:T(1,128)S(1)}, bf16[4,272,384]{2,1,0:T(8,128)(2,1)S(1)}, bf16[4,272,64]{2,1,0:T(8...) custom-call(s32[2]{0:T(128)S(1)} %pad_add_fusion.refs_0_, ...), custom_call_target="tpu_custom_call", output_to_operand_aliasing={{0}: (13, {}), {1}: (14, {}), {2}: (15, {}), {3}: (16, {}),... | custom-call | flops 60000002048 | bytes 18000000 | tf_op jit(solution)/shard_map/pallas_call | solution.py:1161
  38.0 4.1 %shard_map.294 = (bf16[4,256,384]{2,1,0:T(8,128)(2,1)S(1)}, f32[4,256,384]{2,1,0:T(8,128)S(1)}, f32[4,256,64]{2,1,0:T(8,128)S(1)}, f32[8,128]{1,0:T(8,128)S(1)}) custom-call(s32[2]{0:T(128)S(1)} %pad_add_fusion.refs_0_, s32[4,4]{1,0:T(4,128)S(1)} %copy-done.15, ...), custom_call_target="tpu_custom_call" | custom-call | flops 70000001024 | bytes 21000000 | tf_op jit(solution)/shard_map/pallas_call | solution.py:1161
  45.0 2.7 %collective-permute-start.12 = (s16[2,400,128]{2,1,0:T(8,128)(2,1)S(1)}, s16[2,400,128]{2,1,0:T(8,128)(2,1)S(1)}, u32[]{:S(2)}, u32[]{:S(2)}) collective-permute-start(s16[2,400,128]{2,1,0:T(8,128)(2,1)S(1)} %get-tuple-element.237), channel_id=1, source_target_pairs={{0,16},{4,20},{8,24},{12,28},{16,0},{20,4},{24,8},{28,12},{1,17},{... | collective-permute-start | bytes 614408 | tf_op jit(solution)/shard_map/ppermute | solution.py:24
  47.7 3.5 %shard_map.296 = (f32[4,256,384]{2,1,0:T(8,128)S(1)}, f32[8,128]{1,0:T(8,128)S(1)}) custom-call(s32[2]{0:T(128)S(1)} %pad_add_fusion.refs_0_, s32[4,4]{1,0:T(4,128)S(1)} %copy-done.15, bf16[4,256,640]{2,1,0:T(8,128)(2,1)S(1)} %get-tuple-element.223.refs_5_.refs_9_.refs_2_.refs_7_.refs_6_.refs_11_.refs_13_.refs_20_, ...), custom_call_target="tpu_custom_call" | custom-call | flops 60000002048 | bytes 18000000 | tf_op jit(solution)/shard_map/pallas_call | solution.py:1161
  51.2 6.0 %collective-permute-done.12.refs_3_ = s16[2,400,128]{2,1,0:T(8,128)(2,1)S(1)} collective-permute-done((s16[2,400,128]{2,1,0:T(8,128)(2,1)S(1)}, s16[2,400,128]{2,1,0:T(8,128)(2,1)S(1)}, u32[]{:S(2)}, u32[]{:S(2)}) %collective-permute-start.12) | collective-permute-done | bytes 204832 | tf_op jit(solution)/shard_map/ppermute | solution.py:24
  60.4 3.1 %shard_map.298 = (bf16[4,768,256]{2,1,0:T(8,128)(2,1)S(1)}, f32[4,256,384]{2,1,0:T(8,128)S(1)}, f32[8,128]{1,0:T(8,128)S(1)}) custom-call(s32[2]{0:T(128)S(1)} %pad_add_fusion.refs_0_, s32[4,4]{1,0:T(4,128)S(1)} %copy-done.15, bf16[4,192,256]{2,1,0:T(8,128)(2,1)} %bitcast.5.refs_2_.refs_6_, bf16[4,192,256]{2,1,0:T(8,128)(2,1)} %collective-permute-done.14.refs_3_, ...), custom_call_target="tpu_custom_call" | custom-call | flops 54999998464 | bytes 16500000 | tf_op jit(solution)/shard_map/pallas_call | solution.py:1161
  63.5 2.5 %collective-permute-done.13.refs_6_.refs_7_ = s16[2,400,128]{2,1,0:T(8,128)(2,1)S(1)} collective-permute-done((s16[2,400,128]{2,1,0:T(8,128)(2,1)S(1)}, s16[2,400,128]{2,1,0:T(8,128)(2,1)S(1)}, u32[]{:S(2)}, u32[]{:S(2)}) %collective-permute-start.13) | collective-permute-done | bytes 204832 | tf_op jit(solution)/shard_map/ppermute | solution.py:24
  65.9 2.9 %shard_map.299 = (f32[4,256,384]{2,1,0:T(8,128)S(1)}, f32[4,2,256]{2,1,0:T(2,128)S(1)}, f32[8,128]{1,0:T(8,128)S(1)}) custom-call(s32[2]{0:T(128)S(1)} %pad_add_fusion.refs_0_, s32[4,4]{1,0:T(4,128)S(1)} %copy-done.15, bf16[4,256,640]{2,1,0:T(8,128)(2,1)S(1)} %get-tuple-element.223.refs_5_.refs_9_.refs_2_.refs_7_.refs_6_.refs_11_.refs_13_.refs_20_, ...), custom_call_target="tpu_custom_call" | custom-call | flops 65999998976 | bytes 19800000 | tf_op jit(solution)/shard_map/pallas_call | solution.py:1161
  72.8 5.7 %shard_map.300 = (f32[4,256,384]{2,1,0:T(8,128)S(1)}, bf16[4,256,384]{2,1,0:T(8,128)(2,1)S(1)}, bf16[4,256,384]{2,1,0:T(8,128)(2,1)S(1)}, s16[2,400,128]{2,1,0:T...) custom-call(s32[2]{0:T(128)S(1)} %pad_add_fusion.refs_0_, ...), custom_call_target="tpu_custom_call" | custom-call | flops 83000000512 | bytes 24900000 | tf_op jit(solution)/shard_map/pallas_call | solution.py:1161
  80.1 3.9 %shard_map.301 = (f32[4,192,256]{2,1,0:T(8,128)S(1)}, f32[4,192,256]{2,1,0:T(8,128)S(1)}, bf16[4,2,192,256]{3,2,1,0:T(8,128)(2,1)S(1)}, f32[384,384]{1,0:T(8,128...) custom-call(s32[2]{0:T(128)S(1)} %pad_add_fusion.refs_0_, s32[4,4]{1,0:T(4,128)S(1)} %copy-done.15, ...), custom_call_target="tpu_custom_call" | custom-call | flops 67999997952 | bytes 20400000 | tf_op jit(solution)/shard_map/pallas_call | solution.py:1161
  97.5 7.4 %shard_map.306 = (f32[4,256,384]{2,1,0:T(8,128)S(1)}, f32[4,256,256]{2,1,0:T(8,128)S(1)}, f32[4,256,128]{2,1,0:T(8,128)S(1)}, f32[8,128]{1,0:T(8,128)S(1)}) custom-call(s32[2]{0:T(128)S(1)} %pad_add_fusion.refs_0_, s32[4,4]{1,0:T(4,128)S(1)} %copy-done.15, ...), custom_call_target="tpu_custom_call" | custom-call | flops 120000004096 | bytes 36000000 | tf_op jit(solution)/shard_map/pallas_call | solution.py:1161
  112.7 4.0 %shard_map.309 = (f32[4,256,128]{2,1,0:T(8,128)S(1)}, f32[4,256,128]{2,1,0:T(8,128)S(1)}, f32[4,256,384]{2,1,0:T(8,128)S(1)}, f32[4,256,128]{2,1,0:T(8,128)S(1)}...) custom-call(s32[2]{0:T(128)S(1)} %pad_add_fusion.refs_0_, s32[4,4]{1,0:T(4,128)S(1)} %copy-done.15, ...), custom_call_target="tpu_custom_call" | custom-call | flops 64000000000 | bytes 19200000 | tf_op jit(solution)/shard_map/pallas_call | solution.py:1161
  118.2 3.2 %collective-permute-start.31 = (bf16[192,384]{1,0:T(8,128)(2,1)S(1)}, bf16[192,384]{1,0:T(8,128)(2,1)S(1)}, u32[]{:S(2)}, u32[]{:S(2)}) collective-permute-start(bf16[192,384]{1,0:T(8,128)(2,1)S(1)} %get-tuple-element.299), channel_id=1, source_target_pairs={{0,16},{4,20},{8,24},{12,28},{16,0},{20,4},{24,8},{28,12},{1,17},{... | collective-permute-start | bytes 442376 | tf_op jit(solution)/shard_map/ppermute | solution.py:24
  122.7 5.4 %shard_map.312 = (bf16[4,256,384]{2,1,0:T(8,128)(2,1)S(1)}, f32[384,384]{1,0:T(8,128)S(1)}, bf16[384,384]{1,0:T(8,128)(2,1)S(1)}, f32[8,384]{1,0:T(8,128)S(1)}, ...) custom-call(s32[2]{0:T(128)S(1)} %pad_add_fusion.refs_0_, s32[4,4]{1,0:T(4,128)S(1)} %copy-done.15, ...), custom_call_target="tpu_custom_call" | custom-call | flops 70000001024 | bytes 21000000 | tf_op jit(solution)/shard_map/pallas_call | solution.py:1161
  130.9 4.4 %shard_map.314 = (bf16[4,256,128]{2,1,0:T(8,128)(2,1)S(1)}, f32[8,768]{1,0:T(8,128)S(1)}, f32[8,128]{1,0:T(8,128)S(1)}, f32[8,768]{1,0:T(8,128)S(1)}, f32[8,128]{1,0:T(8,128)S(1)}) custom-call(s32[2]{0:T(128)S(1)} %pad_add_fusion.refs_0_, s32[4,4]{1,0:T(4,128)S(1)} %copy-done.15, ...), custom_call_target="tpu_custom_call" | custom-call | flops 60000002048 | bytes 18000000 | tf_op jit(solution)/shard_map/pallas_call | solution.py:1161
  142.3 4.2 %shard_map.317 = (bf16[4,256,64]{2,1,0:T(8,128)(2,1)S(1)}, bf16[4,16,512]{2,1,0:T(8,128)(2,1)S(1)}, bf16[192,384]{1,0:T(8,128)(2,1)S(1)}, f32[32,384]{1,0:T(8,128)S(1)}, f32[8,128]{1,0:T(8,128)S(1)}) custom-call(s32[2]{0:T(128)S(1)} %pad_add_fusion.refs_0_, s32[4,4]{1,0:T(4,128)S(1)} %copy-done.15, f32[2,256,128]{2,1,0:T(8,128)S(1)} %get-tuple-element.310.refs_2_, ...), custom_call_target="tpu_custom_call" | custom-call | flops 49999998976 | bytes 15000000 | tf_op jit(solution)/shard_map/pallas_call | solution.py:1161
  147.8 2.7 %collective-permute-start.38 = (bf16[192,384]{1,0:T(8,128)(2,1)S(1)}, bf16[192,384]{1,0:T(8,128)(2,1)S(1)}, u32[]{:S(2)}, u32[]{:S(2)}) collective-permute-start(bf16[192,384]{1,0:T(8,128)(2,1)S(1)} %get-tuple-element.330.refs_1_), channel_id=1, source_target_pairs={{0,4},{4,0},{8,12},{12,8},{16,20},{20,16},{24,28},{28,24},{1,5},{5... | collective-permute-start | bytes 442376 | tf_op jit(solution)/shard_map/ppermute | solution.py:24
  158.0 3.7 %shard_map.321 = (f32[4,192,256]{2,1,0:T(8,128)S(1)}, f32[4,192,256]{2,1,0:T(8,128)S(1)}, bf16[4,2,208,256]{3,2,1,0:T(8,128)(2,1)S(1)}, f32[4,1,256]{2,1,0:T(1,128)S(1)}, f32[8,128]{1,0:T(8,128)S(1)}) custom-call(s32[2]{0:T(128)S(1)} %pad_add_fusion.refs_0_, s32[4,4]{1,0:T(4,128)S(1)} %copy-done.15, bf16[4,256,384]{2,1,0:T(8,128)(2,1)S(1)} %get-tuple-element.325.refs_2_, ...), custom_call_target="tpu_custom_call" | custom-call | flops 60000002048 | bytes 18000000 | tf_op jit(solution)/shard_map/pallas_call | solution.py:1161
  166.4 3.2 %collective-permute-done.43.refs_2_ = bf16[96,384]{1,0:T(8,128)(2,1)S(1)} collective-permute-done((bf16[96,384]{1,0:T(8,128)(2,1)S(1)}, bf16[96,384]{1,0:T(8,128)(2,1)S(1)}, u32[]{:S(2)}, u32[]{:S(2)}) %collective-permute-start.43) | collective-permute-done | bytes 73760 | tf_op jit(solution)/shard_map/ppermute | solution.py:24
  170.2 2.7 %collective-permute-start.42 = (bf16[192,384]{1,0:T(8,128)(2,1)S(1)}, bf16[192,384]{1,0:T(8,128)(2,1)S(1)}, u32[]{:S(2)}, u32[]{:S(2)}) collective-permute-start(bf16[192,384]{1,0:T(8,128)(2,1)S(1)} %get-tuple-element.351.refs_0_), channel_id=1, source_target_pairs={{0,16},{4,20},{8,24},{12,28},{16,0},{20,4},{24,8},{28,12},{1,17},{... | collective-permute-start | bytes 442376 | tf_op jit(solution)/shard_map/ppermute | solution.py:24
  (213 shorter events, 93.3 us)
Async XLA Ops:
  0.8 15.9 %collective-permute-start.1 = (bf16[4,192,256]{2,1,0:T(8,128)(2,1)}, bf16[4,192,256]{2,1,0:T(8,128)(2,1)S(1)}, u32[]{:S(2)}, u32[]{:S(2)}) collective-permute-start(bf16[4,192,256]{2,1,0:T(8,128)(2,1)} %bitcast.11), channel_id=1, source_target_pairs={{0,2},{1,3},{2,0},{3,1},{4,6},{5,7},{6,4},{7,5},{8,10},{9,11},{10,... | collective-permute-start | bytes 1179656 | tf_op jit(solution)/shard_map/ppermute | solution.py:24
  25.6 9.8 %collective-permute-start.10 = (s16[2,400,128]{2,1,0:T(8,128)(2,1)S(1)}, s16[2,400,128]{2,1,0:T(8,128)(2,1)S(1)}, u32[]{:S(2)}, u32[]{:S(2)}) collective-permute-start(s16[2,400,128]{2,1,0:T(8,128)(2,1)S(1)} %get-tuple-element.226), channel_id=1, source_target_pairs={{0,4},{4,0},{8,12},{12,8},{16,20},{20,16},{24,28},{28,24},{1,5},{5... | collective-permute-start | bytes 614408 | tf_op jit(solution)/shard_map/ppermute | solution.py:24
  34.5 23.9 %collective-permute-start.15 = (bf16[4,192,256]{2,1,0:T(8,128)(2,1)}, bf16[4,192,256]{2,1,0:T(8,128)(2,1)}, u32[]{:S(2)}, u32[]{:S(2)}) collective-permute-start(bf16[4,192,256]{2,1,0:T(8,128)(2,1)} %bitcast.5.refs_2_.refs_6_), channel_id=1, source_target_pairs={{0,2},{1,3},{2,0},{3,1},{4,6},{5,7},{6,4},{7,5},{8,10},{9,11},{10,... | collective-permute-start | bytes 1179656 | tf_op jit(solution)/shard_map/ppermute | solution.py:24
  35.4 24.3 %collective-permute-start.14 = (bf16[4,192,256]{2,1,0:T(8,128)(2,1)}, bf16[4,192,256]{2,1,0:T(8,128)(2,1)}, u32[]{:S(2)}, u32[]{:S(2)}) collective-permute-start(bf16[4,192,256]{2,1,0:T(8,128)(2,1)} %bitcast.5.refs_2_.refs_6_), channel_id=1, source_target_pairs={{0,1},{1,0},{2,3},{3,2},{4,5},{5,4},{6,7},{7,6},{8,9},{9,8},{10,11... | collective-permute-start | bytes 1179656 | tf_op jit(solution)/shard_map/ppermute | solution.py:24
  36.4 7.5 %collective-permute-start.11 = (s16[2,400,128]{2,1,0:T(8,128)(2,1)S(1)}, s16[2,400,128]{2,1,0:T(8,128)(2,1)S(1)}, u32[]{:S(2)}, u32[]{:S(2)}) collective-permute-start(s16[2,400,128]{2,1,0:T(8,128)(2,1)S(1)} %get-tuple-element.229.refs_1_), channel_id=1, source_target_pairs={{0,8},{4,12},{8,0},{12,4},{16,24},{20,28},{24,16},{28,20},{1,9},{5... | collective-permute-start | bytes 614408 | tf_op jit(solution)/shard_map/ppermute | solution.py:24
  45.0 12.2 %collective-permute-start.12 = (s16[2,400,128]{2,1,0:T(8,128)(2,1)S(1)}, s16[2,400,128]{2,1,0:T(8,128)(2,1)S(1)}, u32[]{:S(2)}, u32[]{:S(2)}) collective-permute-start(s16[2,400,128]{2,1,0:T(8,128)(2,1)S(1)} %get-tuple-element.237), channel_id=1, source_target_pairs={{0,16},{4,20},{8,24},{12,28},{16,0},{20,4},{24,8},{28,12},{1,17},{... | collective-permute-start | bytes 614408 | tf_op jit(solution)/shard_map/ppermute | solution.py:24
  84.0 21.0 %collective-permute-start.25 = (bf16[384,384]{1,0:T(8,128)(2,1)}, bf16[384,384]{1,0:T(8,128)(2,1)}, u32[]{:S(2)}, u32[]{:S(2)}) collective-permute-start(bf16[384,384]{1,0:T(8,128)(2,1)} %get-tuple-element.276), channel_id=1, source_target_pairs={{0,4},{4,0},{8,12},{12,8},{16,20},{20,16},{24,28},{28,24},{1,5},{5... | collective-permute-start | bytes 884744 | tf_op jit(solution)/shard_map/ppermute | solution.py:24
  89.1 15.9 %collective-permute-start.26 = (bf16[384,384]{1,0:T(8,128)(2,1)S(1)}, bf16[384,384]{1,0:T(8,128)(2,1)S(1)}, u32[]{:S(2)}, u32[]{:S(2)}) collective-permute-start(bf16[384,384]{1,0:T(8,128)(2,1)S(1)} %get-tuple-element.277), channel_id=1, source_target_pairs={{0,4},{4,0},{8,12},{12,8},{16,20},{20,16},{24,28},{28,24},{1,5},{5... | collective-permute-start | bytes 884744 | tf_op jit(solution)/shard_map/ppermute | solution.py:24
  94.1 11.3 %collective-permute-start.24 = (s16[2,400,128]{2,1,0:T(8,128)(2,1)S(1)}, s16[2,400,128]{2,1,0:T(8,128)(2,1)S(1)}, u32[]{:S(2)}, u32[]{:S(2)}) collective-permute-start(s16[2,400,128]{2,1,0:T(8,128)(2,1)S(1)} %get-tuple-element.273), channel_id=1, source_target_pairs={{0,16},{4,20},{8,24},{12,28},{16,0},{20,4},{24,8},{28,12},{1,17},{... | collective-permute-start | bytes 614408 | tf_op jit(solution)/shard_map/ppermute | solution.py:24
  96.6 25.6 %collective-permute-start.22 = (bf16[4,192,256]{2,1,0:T(8,128)(2,1)}, bf16[4,192,256]{2,1,0:T(8,128)(2,1)}, u32[]{:S(2)}, u32[]{:S(2)}) collective-permute-start(bf16[4,192,256]{2,1,0:T(8,128)(2,1)} %get-tuple-element.267), channel_id=1, source_target_pairs={{0,2},{1,3},{2,0},{3,1},{4,6},{5,7},{6,4},{7,5},{8,10},{9,11},{10,... | collective-permute-start | bytes 1179656 | tf_op jit(solution)/shard_map/ppermute | solution.py:24
  109.7 7.8 %collective-permute-start.29 = (bf16[384,384]{1,0:T(8,128)(2,1)S(1)}, bf16[384,384]{1,0:T(8,128)(2,1)S(1)}, u32[]{:S(2)}, u32[]{:S(2)}) collective-permute-start(bf16[384,384]{1,0:T(8,128)(2,1)S(1)} %get-tuple-element.292), channel_id=1, source_target_pairs={{0,8},{4,12},{8,0},{12,4},{16,24},{20,28},{24,16},{28,20},{1,9},{5... | collective-permute-start | bytes 884744 | tf_op jit(solution)/shard_map/ppermute | solution.py:24
  118.2 9.9 %collective-permute-start.31 = (bf16[192,384]{1,0:T(8,128)(2,1)S(1)}, bf16[192,384]{1,0:T(8,128)(2,1)S(1)}, u32[]{:S(2)}, u32[]{:S(2)}) collective-permute-start(bf16[192,384]{1,0:T(8,128)(2,1)S(1)} %get-tuple-element.299), channel_id=1, source_target_pairs={{0,16},{4,20},{8,24},{12,28},{16,0},{20,4},{24,8},{28,12},{1,17},{... | collective-permute-start | bytes 442376 | tf_op jit(solution)/shard_map/ppermute | solution.py:24
  128.7 9.0 %collective-permute-start.32 = (bf16[192,384]{1,0:T(8,128)(2,1)S(1)}, bf16[192,384]{1,0:T(8,128)(2,1)S(1)}, u32[]{:S(2)}, u32[]{:S(2)}) collective-permute-start(bf16[192,384]{1,0:T(8,128)(2,1)S(1)} %get-tuple-element.301.refs_1_), channel_id=1, source_target_pairs={{0,16},{4,20},{8,24},{12,28},{16,0},{20,4},{24,8},{28,12},{1,17},{... | collective-permute-start | bytes 442376 | tf_op jit(solution)/shard_map/ppermute | solution.py:24
  128.8 13.4 %collective-permute-start.34 = (f32[2,256,128]{2,1,0:T(8,128)S(1)}, f32[2,256,128]{2,1,0:T(8,128)S(1)}, u32[]{:S(2)}, u32[]{:S(2)}) collective-permute-start(f32[2,256,128]{2,1,0:T(8,128)S(1)} %get-tuple-element.311), channel_id=1, source_target_pairs={{0,2},{1,3},{2,0},{3,1},{4,6},{5,7},{6,4},{7,5},{8,10},{9,11},{10,... | collective-permute-start | bytes 786440 | tf_op jit(solution)/shard_map/ppermute | solution.py:24
  129.7 9.5 %collective-permute-start.30 = (bf16[384,384]{1,0:T(8,128)(2,1)S(1)}, bf16[384,384]{1,0:T(8,128)(2,1)S(1)}, u32[]{:S(2)}, u32[]{:S(2)}) collective-permute-start(bf16[384,384]{1,0:T(8,128)(2,1)S(1)} %get-tuple-element.297), channel_id=1, source_target_pairs={{0,4},{4,0},{8,12},{12,8},{16,20},{20,16},{24,28},{28,24},{1,5},{5... | collective-permute-start | bytes 884744 | tf_op jit(solution)/shard_map/ppermute | solution.py:24
  138.3 18.2 %collective-permute-start.37 = (bf16[384,384]{1,0:T(8,128)(2,1)S(1)}, bf16[384,384]{1,0:T(8,128)(2,1)S(1)}, u32[]{:S(2)}, u32[]{:S(2)}) collective-permute-start(bf16[384,384]{1,0:T(8,128)(2,1)S(1)} %get-tuple-element.329.refs_1_), channel_id=1, source_target_pairs={{0,8},{4,12},{8,0},{12,4},{16,24},{20,28},{24,16},{28,20},{1,9},{5... | collective-permute-start | bytes 884744 | tf_op jit(solution)/shard_map/ppermute | solution.py:24
  139.9 10.6 %collective-permute-start.33 = (bf16[192,384]{1,0:T(8,128)(2,1)S(1)}, bf16[192,384]{1,0:T(8,128)(2,1)S(1)}, u32[]{:S(2)}, u32[]{:S(2)}) collective-permute-start(bf16[192,384]{1,0:T(8,128)(2,1)S(1)} %get-tuple-element.309), channel_id=1, source_target_pairs={{0,8},{4,12},{8,0},{12,4},{16,24},{20,28},{24,16},{28,20},{1,9},{5... | collective-permute-start | bytes 442376 | tf_op jit(solution)/shard_map/ppermute | solution.py:24
  146.5 11.3 %collective-permute-start.36 = (bf16[4,16,512]{2,1,0:T(8,128)(2,1)S(1)}, bf16[4,16,512]{2,1,0:T(8,128)(2,1)S(1)}, u32[]{:S(2)}, u32[]{:S(2)}) collective-permute-start(bf16[4,16,512]{2,1,0:T(8,128)(2,1)S(1)} %get-tuple-element.326), channel_id=1, source_target_pairs={{4,0},{8,4},{12,8},{16,12},{20,16},{24,20},{28,24},{5,1},{9,5},{13... | collective-permute-start | bytes 196616 | tf_op jit(solution)/shard_map/ppermute | solution.py:24
  151.1 10.7 %collective-permute-start.35 = (bf16[96,384]{1,0:T(8,128)(2,1)S(1)}, bf16[96,384]{1,0:T(8,128)(2,1)S(1)}, u32[]{:S(2)}, u32[]{:S(2)}) collective-permute-start(bf16[96,384]{1,0:T(8,128)(2,1)S(1)} %get-tuple-element.324), channel_id=1, source_target_pairs={{0,16},{4,20},{8,24},{12,28},{16,0},{20,4},{24,8},{28,12},{1,17},{... | collective-permute-start | bytes 221192 | tf_op jit(solution)/shard_map/ppermute | solution.py:24
  157.2 16.7 %collective-permute-start.45 = (bf16[768,384]{1,0:T(8,128)(2,1)S(1)}, bf16[768,384]{1,0:T(8,128)(2,1)S(1)}, u32[]{:S(2)}, u32[]{:S(2)}) collective-permute-start(bf16[768,384]{1,0:T(8,128)(2,1)S(1)} %get-tuple-element.356.refs_1_), channel_id=1, source_target_pairs={{0,4},{4,0},{8,12},{12,8},{16,20},{20,16},{24,28},{28,24},{1,5},{5... | collective-permute-start | bytes 1769480 | tf_op jit(solution)/shard_map/ppermute | solution.py:24
  170.2 8.4 %collective-permute-start.44 = (bf16[192,384]{1,0:T(8,128)(2,1)S(1)}, bf16[192,384]{1,0:T(8,128)(2,1)S(1)}, u32[]{:S(2)}, u32[]{:S(2)}) collective-permute-start(bf16[192,384]{1,0:T(8,128)(2,1)S(1)} %get-tuple-element.355.refs_1_), channel_id=1, source_target_pairs={{0,8},{4,12},{8,0},{12,4},{16,24},{20,28},{24,16},{28,20},{1,9},{5... | collective-permute-start | bytes 442376 | tf_op jit(solution)/shard_map/ppermute | solution.py:24
  170.2 9.6 %collective-permute-start.42 = (bf16[192,384]{1,0:T(8,128)(2,1)S(1)}, bf16[192,384]{1,0:T(8,128)(2,1)S(1)}, u32[]{:S(2)}, u32[]{:S(2)}) collective-permute-start(bf16[192,384]{1,0:T(8,128)(2,1)S(1)} %get-tuple-element.351.refs_0_), channel_id=1, source_target_pairs={{0,16},{4,20},{8,24},{12,28},{16,0},{20,4},{24,8},{28,12},{1,17},{... | collective-permute-start | bytes 442376 | tf_op jit(solution)/shard_map/ppermute | solution.py:24
  172.9 11.1 %collective-permute-start.41 = (bf16[4,208,256]{2,1,0:T(8,128)(2,1)S(1)}, bf16[4,208,256]{2,1,0:T(8,128)(2,1)S(1)}, u32[]{:S(2)}, u32[]{:S(2)}) collective-permute-start(bf16[4,208,256]{2,1,0:T(8,128)(2,1)S(1)} %get-tuple-element.345), channel_id=1, source_target_pairs={{0,2},{1,3},{2,0},{3,1},{4,6},{5,7},{6,4},{7,5},{8,10},{9,11},{10,... | collective-permute-start | bytes 1277960 | tf_op jit(solution)/shard_map/ppermute | solution.py:24
  180.6 9.4 %collective-permute-start.48 = (bf16[384,384]{1,0:T(8,128)(2,1)S(1)}, bf16[384,384]{1,0:T(8,128)(2,1)S(1)}, u32[]{:S(2)}, u32[]{:S(2)}) collective-permute-start(bf16[384,384]{1,0:T(8,128)(2,1)S(1)} %get-tuple-element.367.refs_1_), channel_id=1, source_target_pairs={{0,4},{4,0},{8,12},{12,8},{16,20},{20,16},{24,28},{28,24},{1,5},{5... | collective-permute-start | bytes 884744 | tf_op jit(solution)/shard_map/ppermute | solution.py:24
  (70 other events, 415.5 us)

commit v2 on v1

--- a/solution.py
+++ b/solution.py
@@ -1518,7 +1518,7 @@
 
     gy, gated, ggate, gkeep, gsend, gate_small = call(
         functools.partial(grad_kernel, dims, total_inner),
-        grid,
+        (packs // half,),
         [
             *[pack_spec((2, count))] * 4, xbc_spec, lane_spec, chan_spec, chan_spec, chan_spec, vec,
             vec,
@@ -1529,7 +1529,7 @@
         [],
         pre,
         *stats, xbc, steps, y, gate, gg, gain_gate, skip,
-        us=8.3,
+        us=8.3, group=half,
     )
 
     piece_shape = shape(packs, part, count, f32)
@@ -1579,7 +1579,7 @@
     def diag_work(_):
         kept["diag"] = call(
             functools.partial(diag_kernel, dims),
-            grid,
+            (packs // half,),
             [xbc_spec, lane_spec, chan_spec, chan_spec, state_spec, state_spec],
             [chan_spec, pack_spec((count, bc)), lane_spec],
             [
@@ -1589,7 +1589,7 @@
             [],
             pre,
             xbc, steps, gy, y, state_keep, state_recv,
-            us=12,
+            us=12, group=half,
         )
 
     def early_work(_):
@@ -1639,7 +1639,7 @@
 
     main_x, keep, give, grad_conv, gain_x = call(
         functools.partial(xback_kernel, dims),
-        grid,
+        (packs // half,),
         [
             chan_spec, pack_spec((ext, inner)), model_spec, whole_spec((features, LANES)),
             pack_spec(edge_tile), whole_spec((8, inner)), square,
@@ -1652,7 +1652,7 @@
         ],
         pre,
         grad_x, raw_x, normed, edge, edge_x, conv_own, proj_x,
-        us=7, wait=(out_far,),
+        us=7, group=half, wait=(out_far,),
     )
     late_sum.put(keep, give)
     advance(early_sum, meta)

time: 192 us -> 191 us (level)
  transfers between devices with their start and end apart: 49 -> 49, of which waited for: 23 -> 24; matrix products, arithmetic and copies ran while one was open for 0% -> 0% of each run, Pallas kernels for 42% -> 42%
where the time goes in v2:
time: 191 us; the launch traced here: 190 us
  Pallas kernels  95.8 us (50%)
  starting transfers between devices  53.5 us (28%)
  waiting for transfers between devices  38.1 us (20%)
    pallas_call x48, Pallas kernels, call(): pl.pallas_call(body, grid_spec=pltpu.PrefetchScalarGridSpec(num_scalar_pr...  95.8 us
    ppermute x49, starting transfers between devices, permuted(): y = lax.ppermute(x, axis, route)  53.5 us
    ppermute x49, waiting for transfers between devices, permuted(): y = lax.ppermute(x, axis, route)  38.1 us
  transfers between devices with their start and end apart: 49, of which 24 were waited for; matrix products, arithmetic and copies ran while one was open for 0% of the time, Pallas kernels for 42%

profile of v2, /device:TPU:0, one launch (start us, length us, event | category | flops | bytes accessed | tf_op | source)
XLA Modules:
  0.0 190.3 jit_solution(11434333070842894440)
XLA Ops:
  0.8 3.0 %collective-permute-start.1 = (bf16[4,192,256]{2,1,0:T(8,128)(2,1)}, bf16[4,192,256]{2,1,0:T(8,128)(2,1)S(1)}, u32[]{:S(2)}, u32[]{:S(2)}) collective-permute-start(bf16[4,192,256]{2,1,0:T(8,128)(2,1)} %bitcast.11), channel_id=1, source_target_pairs={{0,2},{1,3},{2,0},{3,1},{4,6},{5,7},{6,4},{7,5},{8,10},{9,11},{10,... | collective-permute-start | bytes 1179656 | tf_op jit(solution)/shard_map/ppermute | solution.py:24
  5.5 3.4 %collective-permute-start.2 = (bf16[192,128]{1,0:T(8,128)(2,1)S(1)}, bf16[192,128]{1,0:T(8,128)(2,1)S(1)}, u32[]{:S(2)}, u32[]{:S(2)}) collective-permute-start(bf16[192,128]{1,0:T(8,128)(2,1)S(1)} %get-tuple-element.201), channel_id=1, source_target_pairs={{0,4},{4,8},{8,12},{12,16},{16,20},{20,24},{24,28},{1,5},{5,9},{9,... | collective-permute-start | bytes 147464 | tf_op jit(solution)/shard_map/ppermute | solution.py:24
  13.2 3.4 %collective-permute-done.3.refs_3_ = bf16[192,128]{1,0:T(8,128)(2,1)S(1)} collective-permute-done((bf16[192,128]{1,0:T(8,128)(2,1)S(1)}, bf16[192,128]{1,0:T(8,128)(2,1)S(1)}, u32[]{:S(2)}, u32[]{:S(2)}) %collective-permute-start.3) | collective-permute-done | bytes 49184 | tf_op jit(solution)/shard_map/ppermute | solution.py:24
  19.8 5.9 %shard_map.291 = (bf16[4,768,256]{2,1,0:T(8,128)(2,1)S(1)}, f32[4,1,256]{2,1,0:T(1,128)S(1)}, bf16[4,272,384]{2,1,0:T(8,128)(2,1)S(1)}, bf16[4,272,64]{2,1,0:T(8...) custom-call(s32[2]{0:T(128)S(1)} %pad_add_fusion.refs_0_, ...), custom_call_target="tpu_custom_call" | custom-call | flops 60000002048 | bytes 18000000 | tf_op jit(solution)/shard_map/pallas_call | solution.py:1161
  28.0 5.9 %shard_map.292 = (bf16[4,768,256]{2,1,0:T(8,128)(2,1)S(1)}, f32[4,1,256]{2,1,0:T(1,128)S(1)}, bf16[4,272,384]{2,1,0:T(8,128)(2,1)S(1)}, bf16[4,272,64]{2,1,0:T(8...) custom-call(s32[2]{0:T(128)S(1)} %pad_add_fusion.refs_0_, ...), custom_call_target="tpu_custom_call", output_to_operand_aliasing={{0}: (13, {}), {1}: (14, {}), {2}: (15, {}), {3}: (16, {}),... | custom-call | flops 60000002048 | bytes 18000000 | tf_op jit(solution)/shard_map/pallas_call | solution.py:1161
  38.0 4.1 %shard_map.294 = (bf16[4,256,384]{2,1,0:T(8,128)(2,1)S(1)}, f32[4,256,384]{2,1,0:T(8,128)S(1)}, f32[4,256,64]{2,1,0:T(8,128)S(1)}, f32[8,128]{1,0:T(8,128)S(1)}) custom-call(s32[2]{0:T(128)S(1)} %pad_add_fusion.refs_0_, s32[4,4]{1,0:T(4,128)S(1)} %copy-done.15, ...), custom_call_target="tpu_custom_call" | custom-call | flops 70000001024 | bytes 21000000 | tf_op jit(solution)/shard_map/pallas_call | solution.py:1161
  45.0 2.7 %collective-permute-start.12 = (s16[2,400,128]{2,1,0:T(8,128)(2,1)S(1)}, s16[2,400,128]{2,1,0:T(8,128)(2,1)S(1)}, u32[]{:S(2)}, u32[]{:S(2)}) collective-permute-start(s16[2,400,128]{2,1,0:T(8,128)(2,1)S(1)} %get-tuple-element.237), channel_id=1, source_target_pairs={{0,16},{4,20},{8,24},{12,28},{16,0},{20,4},{24,8},{28,12},{1,17},{... | collective-permute-start | bytes 614408 | tf_op jit(solution)/shard_map/ppermute | solution.py:24
  47.7 3.5 %shard_map.296 = (f32[4,256,384]{2,1,0:T(8,128)S(1)}, f32[8,128]{1,0:T(8,128)S(1)}) custom-call(s32[2]{0:T(128)S(1)} %pad_add_fusion.refs_0_, s32[4,4]{1,0:T(4,128)S(1)} %copy-done.15, bf16[4,256,640]{2,1,0:T(8,128)(2,1)S(1)} %get-tuple-element.223.refs_5_.refs_9_.refs_2_.refs_7_.refs_6_.refs_11_.refs_13_.refs_20_, ...), custom_call_target="tpu_custom_call" | custom-call | flops 60000002048 | bytes 18000000 | tf_op jit(solution)/shard_map/pallas_call | solution.py:1161
  51.2 6.0 %collective-permute-done.12.refs_3_ = s16[2,400,128]{2,1,0:T(8,128)(2,1)S(1)} collective-permute-done((s16[2,400,128]{2,1,0:T(8,128)(2,1)S(1)}, s16[2,400,128]{2,1,0:T(8,128)(2,1)S(1)}, u32[]{:S(2)}, u32[]{:S(2)}) %collective-permute-start.12) | collective-permute-done | bytes 204832 | tf_op jit(solution)/shard_map/ppermute | solution.py:24
  60.4 3.1 %shard_map.298 = (bf16[4,768,256]{2,1,0:T(8,128)(2,1)S(1)}, f32[4,256,384]{2,1,0:T(8,128)S(1)}, f32[8,128]{1,0:T(8,128)S(1)}) custom-call(s32[2]{0:T(128)S(1)} %pad_add_fusion.refs_0_, s32[4,4]{1,0:T(4,128)S(1)} %copy-done.15, bf16[4,192,256]{2,1,0:T(8,128)(2,1)} %bitcast.5.refs_2_.refs_6_, bf16[4,192,256]{2,1,0:T(8,128)(2,1)} %collective-permute-done.14.refs_3_, ...), custom_call_target="tpu_custom_call" | custom-call | flops 54999998464 | bytes 16500000 | tf_op jit(solution)/shard_map/pallas_call | solution.py:1161
  65.9 2.9 %shard_map.299 = (f32[4,256,384]{2,1,0:T(8,128)S(1)}, f32[4,2,256]{2,1,0:T(2,128)S(1)}, f32[8,128]{1,0:T(8,128)S(1)}) custom-call(s32[2]{0:T(128)S(1)} %pad_add_fusion.refs_0_, s32[4,4]{1,0:T(4,128)S(1)} %copy-done.15, bf16[4,256,640]{2,1,0:T(8,128)(2,1)S(1)} %get-tuple-element.223.refs_5_.refs_9_.refs_2_.refs_7_.refs_6_.refs_11_.refs_13_.refs_20_, ...), custom_call_target="tpu_custom_call" | custom-call | flops 65999998976 | bytes 19800000 | tf_op jit(solution)/shard_map/pallas_call | solution.py:1161
  72.8 5.4 %shard_map.300 = (f32[4,256,384]{2,1,0:T(8,128)S(1)}, bf16[4,256,384]{2,1,0:T(8,128)(2,1)S(1)}, bf16[4,256,384]{2,1,0:T(8,128)(2,1)S(1)}, s16[2,400,128]{2,1,0:T...) custom-call(s32[2]{0:T(128)S(1)} %pad_add_fusion.refs_0_, ...), custom_call_target="tpu_custom_call" | custom-call | flops 83000000512 | bytes 24900000 | tf_op jit(solution)/shard_map/pallas_call | solution.py:1161
  79.8 3.7 %shard_map.301 = (f32[4,192,256]{2,1,0:T(8,128)S(1)}, f32[4,192,256]{2,1,0:T(8,128)S(1)}, bf16[4,2,192,256]{3,2,1,0:T(8,128)(2,1)S(1)}, f32[384,384]{1,0:T(8,128...) custom-call(s32[2]{0:T(128)S(1)} %pad_add_fusion.refs_0_, s32[4,4]{1,0:T(4,128)S(1)} %copy-done.15, ...), custom_call_target="tpu_custom_call" | custom-call | flops 67999997952 | bytes 20400000 | tf_op jit(solution)/shard_map/pallas_call | solution.py:1161
  93.6 2.8 %collective-permute-start.24 = (s16[2,400,128]{2,1,0:T(8,128)(2,1)S(1)}, s16[2,400,128]{2,1,0:T(8,128)(2,1)S(1)}, u32[]{:S(2)}, u32[]{:S(2)}) collective-permute-start(s16[2,400,128]{2,1,0:T(8,128)(2,1)S(1)} %get-tuple-element.273), channel_id=1, source_target_pairs={{0,16},{4,20},{8,24},{12,28},{16,0},{20,4},{24,8},{28,12},{1,17},{... | collective-permute-start | bytes 614408 | tf_op jit(solution)/shard_map/ppermute | solution.py:24
  97.0 6.7 %shard_map.306 = (f32[4,256,384]{2,1,0:T(8,128)S(1)}, f32[4,256,256]{2,1,0:T(8,128)S(1)}, f32[4,256,128]{2,1,0:T(8,128)S(1)}, f32[8,128]{1,0:T(8,128)S(1)}) custom-call(s32[2]{0:T(128)S(1)} %pad_add_fusion.refs_0_, s32[4,4]{1,0:T(4,128)S(1)} %copy-done.15, ...), custom_call_target="tpu_custom_call" | custom-call | flops 120000004096 | bytes 36000000 | tf_op jit(solution)/shard_map/pallas_call | solution.py:1161
  112.4 4.0 %shard_map.309 = (f32[4,256,128]{2,1,0:T(8,128)S(1)}, f32[4,256,128]{2,1,0:T(8,128)S(1)}, f32[4,256,384]{2,1,0:T(8,128)S(1)}, f32[4,256,128]{2,1,0:T(8,128)S(1)}...) custom-call(s32[2]{0:T(128)S(1)} %pad_add_fusion.refs_0_, s32[4,4]{1,0:T(4,128)S(1)} %copy-done.15, ...), custom_call_target="tpu_custom_call" | custom-call | flops 64000000000 | bytes 19200000 | tf_op jit(solution)/shard_map/pallas_call | solution.py:1161
  117.3 3.1 %collective-permute-start.31 = (bf16[192,384]{1,0:T(8,128)(2,1)S(1)}, bf16[192,384]{1,0:T(8,128)(2,1)S(1)}, u32[]{:S(2)}, u32[]{:S(2)}) collective-permute-start(bf16[192,384]{1,0:T(8,128)(2,1)S(1)} %get-tuple-element.299), channel_id=1, source_target_pairs={{0,16},{4,20},{8,24},{12,28},{16,0},{20,4},{24,8},{28,12},{1,17},{... | collective-permute-start | bytes 442376 | tf_op jit(solution)/shard_map/ppermute | solution.py:24
  121.8 5.4 %shard_map.312 = (bf16[4,256,384]{2,1,0:T(8,128)(2,1)S(1)}, f32[384,384]{1,0:T(8,128)S(1)}, bf16[384,384]{1,0:T(8,128)(2,1)S(1)}, f32[8,384]{1,0:T(8,128)S(1)}, ...) custom-call(s32[2]{0:T(128)S(1)} %pad_add_fusion.refs_0_, s32[4,4]{1,0:T(4,128)S(1)} %copy-done.15, ...), custom_call_target="tpu_custom_call" | custom-call | flops 70000001024 | bytes 21000000 | tf_op jit(solution)/shard_map/pallas_call | solution.py:1161
  130.2 4.4 %shard_map.314 = (bf16[4,256,128]{2,1,0:T(8,128)(2,1)S(1)}, f32[8,768]{1,0:T(8,128)S(1)}, f32[8,128]{1,0:T(8,128)S(1)}, f32[8,768]{1,0:T(8,128)S(1)}, f32[8,128]{1,0:T(8,128)S(1)}) custom-call(s32[2]{0:T(128)S(1)} %pad_add_fusion.refs_0_, s32[4,4]{1,0:T(4,128)S(1)} %copy-done.15, ...), custom_call_target="tpu_custom_call" | custom-call | flops 60000002048 | bytes 18000000 | tf_op jit(solution)/shard_map/pallas_call | solution.py:1161
  134.6 2.7 %collective-permute-done.32.refs_2_ = bf16[192,384]{1,0:T(8,128)(2,1)S(1)} collective-permute-done((bf16[192,384]{1,0:T(8,128)(2,1)S(1)}, bf16[192,384]{1,0:T(8,128)(2,1)S(1)}, u32[]{:S(2)}, u32[]{:S(2)}) %collective-permute-start.32) | collective-permute-done | bytes 147488 | tf_op jit(solution)/shard_map/ppermute | solution.py:24
  141.5 4.0 %shard_map.317 = (bf16[4,256,64]{2,1,0:T(8,128)(2,1)S(1)}, bf16[4,16,512]{2,1,0:T(8,128)(2,1)S(1)}, bf16[192,384]{1,0:T(8,128)(2,1)S(1)}, f32[32,384]{1,0:T(8,128)S(1)}, f32[8,128]{1,0:T(8,128)S(1)}) custom-call(s32[2]{0:T(128)S(1)} %pad_add_fusion.refs_0_, s32[4,4]{1,0:T(4,128)S(1)} %copy-done.15, f32[2,256,128]{2,1,0:T(8,128)S(1)} %get-tuple-element.310.refs_2_, ...), custom_call_target="tpu_custom_call" | custom-call | flops 49999998976 | bytes 15000000 | tf_op jit(solution)/shard_map/pallas_call | solution.py:1161
  146.8 2.7 %collective-permute-start.38 = (bf16[192,384]{1,0:T(8,128)(2,1)S(1)}, bf16[192,384]{1,0:T(8,128)(2,1)S(1)}, u32[]{:S(2)}, u32[]{:S(2)}) collective-permute-start(bf16[192,384]{1,0:T(8,128)(2,1)S(1)} %get-tuple-element.330.refs_1_), channel_id=1, source_target_pairs={{0,4},{4,0},{8,12},{12,8},{16,20},{20,16},{24,28},{28,24},{1,5},{5... | collective-permute-start | bytes 442376 | tf_op jit(solution)/shard_map/ppermute | solution.py:24
  156.9 3.7 %shard_map.321 = (f32[4,192,256]{2,1,0:T(8,128)S(1)}, f32[4,192,256]{2,1,0:T(8,128)S(1)}, bf16[4,2,208,256]{3,2,1,0:T(8,128)(2,1)S(1)}, f32[4,1,256]{2,1,0:T(1,128)S(1)}, f32[8,128]{1,0:T(8,128)S(1)}) custom-call(s32[2]{0:T(128)S(1)} %pad_add_fusion.refs_0_, s32[4,4]{1,0:T(4,128)S(1)} %copy-done.15, bf16[4,256,384]{2,1,0:T(8,128)(2,1)S(1)} %get-tuple-element.325.refs_2_, ...), custom_call_target="tpu_custom_call" | custom-call | flops 60000002048 | bytes 18000000 | tf_op jit(solution)/shard_map/pallas_call | solution.py:1161
  165.5 3.1 %collective-permute-done.43.refs_2_ = bf16[96,384]{1,0:T(8,128)(2,1)S(1)} collective-permute-done((bf16[96,384]{1,0:T(8,128)(2,1)S(1)}, bf16[96,384]{1,0:T(8,128)(2,1)S(1)}, u32[]{:S(2)}, u32[]{:S(2)}) %collective-permute-start.43) | collective-permute-done | bytes 73760 | tf_op jit(solution)/shard_map/ppermute | solution.py:24
  (213 shorter events, 93.5 us)
Async XLA Ops:
  0.8 15.9 %collective-permute-start.1 = (bf16[4,192,256]{2,1,0:T(8,128)(2,1)}, bf16[4,192,256]{2,1,0:T(8,128)(2,1)S(1)}, u32[]{:S(2)}, u32[]{:S(2)}) collective-permute-start(bf16[4,192,256]{2,1,0:T(8,128)(2,1)} %bitcast.11), channel_id=1, source_target_pairs={{0,2},{1,3},{2,0},{3,1},{4,6},{5,7},{6,4},{7,5},{8,10},{9,11},{10,... | collective-permute-start | bytes 1179656 | tf_op jit(solution)/shard_map/ppermute | solution.py:24
  25.6 9.8 %collective-permute-start.10 = (s16[2,400,128]{2,1,0:T(8,128)(2,1)S(1)}, s16[2,400,128]{2,1,0:T(8,128)(2,1)S(1)}, u32[]{:S(2)}, u32[]{:S(2)}) collective-permute-start(s16[2,400,128]{2,1,0:T(8,128)(2,1)S(1)} %get-tuple-element.226), channel_id=1, source_target_pairs={{0,4},{4,0},{8,12},{12,8},{16,20},{20,16},{24,28},{28,24},{1,5},{5... | collective-permute-start | bytes 614408 | tf_op jit(solution)/shard_map/ppermute | solution.py:24
  34.5 23.9 %collective-permute-start.15 = (bf16[4,192,256]{2,1,0:T(8,128)(2,1)}, bf16[4,192,256]{2,1,0:T(8,128)(2,1)}, u32[]{:S(2)}, u32[]{:S(2)}) collective-permute-start(bf16[4,192,256]{2,1,0:T(8,128)(2,1)} %bitcast.5.refs_2_.refs_6_), channel_id=1, source_target_pairs={{0,2},{1,3},{2,0},{3,1},{4,6},{5,7},{6,4},{7,5},{8,10},{9,11},{10,... | collective-permute-start | bytes 1179656 | tf_op jit(solution)/shard_map/ppermute | solution.py:24
  35.4 24.3 %collective-permute-start.14 = (bf16[4,192,256]{2,1,0:T(8,128)(2,1)}, bf16[4,192,256]{2,1,0:T(8,128)(2,1)}, u32[]{:S(2)}, u32[]{:S(2)}) collective-permute-start(bf16[4,192,256]{2,1,0:T(8,128)(2,1)} %bitcast.5.refs_2_.refs_6_), channel_id=1, source_target_pairs={{0,1},{1,0},{2,3},{3,2},{4,5},{5,4},{6,7},{7,6},{8,9},{9,8},{10,11... | collective-permute-start | bytes 1179656 | tf_op jit(solution)/shard_map/ppermute | solution.py:24
  36.4 7.5 %collective-permute-start.11 = (s16[2,400,128]{2,1,0:T(8,128)(2,1)S(1)}, s16[2,400,128]{2,1,0:T(8,128)(2,1)S(1)}, u32[]{:S(2)}, u32[]{:S(2)}) collective-permute-start(s16[2,400,128]{2,1,0:T(8,128)(2,1)S(1)} %get-tuple-element.229.refs_1_), channel_id=1, source_target_pairs={{0,8},{4,12},{8,0},{12,4},{16,24},{20,28},{24,16},{28,20},{1,9},{5... | collective-permute-start | bytes 614408 | tf_op jit(solution)/shard_map/ppermute | solution.py:24
  45.0 12.2 %collective-permute-start.12 = (s16[2,400,128]{2,1,0:T(8,128)(2,1)S(1)}, s16[2,400,128]{2,1,0:T(8,128)(2,1)S(1)}, u32[]{:S(2)}, u32[]{:S(2)}) collective-permute-start(s16[2,400,128]{2,1,0:T(8,128)(2,1)S(1)} %get-tuple-element.237), channel_id=1, source_target_pairs={{0,16},{4,20},{8,24},{12,28},{16,0},{20,4},{24,8},{28,12},{1,17},{... | collective-permute-start | bytes 614408 | tf_op jit(solution)/shard_map/ppermute | solution.py:24
  83.4 20.4 %collective-permute-start.25 = (bf16[384,384]{1,0:T(8,128)(2,1)}, bf16[384,384]{1,0:T(8,128)(2,1)}, u32[]{:S(2)}, u32[]{:S(2)}) collective-permute-start(bf16[384,384]{1,0:T(8,128)(2,1)} %get-tuple-element.276), channel_id=1, source_target_pairs={{0,4},{4,0},{8,12},{12,8},{16,20},{20,16},{24,28},{28,24},{1,5},{5... | collective-permute-start | bytes 884744 | tf_op jit(solution)/shard_map/ppermute | solution.py:24
  88.8 15.0 %collective-permute-start.26 = (bf16[384,384]{1,0:T(8,128)(2,1)S(1)}, bf16[384,384]{1,0:T(8,128)(2,1)S(1)}, u32[]{:S(2)}, u32[]{:S(2)}) collective-permute-start(bf16[384,384]{1,0:T(8,128)(2,1)S(1)} %get-tuple-element.277), channel_id=1, source_target_pairs={{0,4},{4,0},{8,12},{12,8},{16,20},{20,16},{24,28},{28,24},{1,5},{5... | collective-permute-start | bytes 884744 | tf_op jit(solution)/shard_map/ppermute | solution.py:24
  93.6 11.2 %collective-permute-start.24 = (s16[2,400,128]{2,1,0:T(8,128)(2,1)S(1)}, s16[2,400,128]{2,1,0:T(8,128)(2,1)S(1)}, u32[]{:S(2)}, u32[]{:S(2)}) collective-permute-start(s16[2,400,128]{2,1,0:T(8,128)(2,1)S(1)} %get-tuple-element.273), channel_id=1, source_target_pairs={{0,16},{4,20},{8,24},{12,28},{16,0},{20,4},{24,8},{28,12},{1,17},{... | collective-permute-start | bytes 614408 | tf_op jit(solution)/shard_map/ppermute | solution.py:24
  96.4 24.9 %collective-permute-start.22 = (bf16[4,192,256]{2,1,0:T(8,128)(2,1)}, bf16[4,192,256]{2,1,0:T(8,128)(2,1)}, u32[]{:S(2)}, u32[]{:S(2)}) collective-permute-start(bf16[4,192,256]{2,1,0:T(8,128)(2,1)} %get-tuple-element.267), channel_id=1, source_target_pairs={{0,2},{1,3},{2,0},{3,1},{4,6},{5,7},{6,4},{7,5},{8,10},{9,11},{10,... | collective-permute-start | bytes 1179656 | tf_op jit(solution)/shard_map/ppermute | solution.py:24
  108.8 7.8 %collective-permute-start.29 = (bf16[384,384]{1,0:T(8,128)(2,1)S(1)}, bf16[384,384]{1,0:T(8,128)(2,1)S(1)}, u32[]{:S(2)}, u32[]{:S(2)}) collective-permute-start(bf16[384,384]{1,0:T(8,128)(2,1)S(1)} %get-tuple-element.292), channel_id=1, source_target_pairs={{0,8},{4,12},{8,0},{12,4},{16,24},{20,28},{24,16},{28,20},{1,9},{5... | collective-permute-start | bytes 884744 | tf_op jit(solution)/shard_map/ppermute | solution.py:24
  117.3 10.2 %collective-permute-start.31 = (bf16[192,384]{1,0:T(8,128)(2,1)S(1)}, bf16[192,384]{1,0:T(8,128)(2,1)S(1)}, u32[]{:S(2)}, u32[]{:S(2)}) collective-permute-start(bf16[192,384]{1,0:T(8,128)(2,1)S(1)} %get-tuple-element.299), channel_id=1, source_target_pairs={{0,16},{4,20},{8,24},{12,28},{16,0},{20,4},{24,8},{28,12},{1,17},{... | collective-permute-start | bytes 442376 | tf_op jit(solution)/shard_map/ppermute | solution.py:24
  128.1 9.2 %collective-permute-start.32 = (bf16[192,384]{1,0:T(8,128)(2,1)S(1)}, bf16[192,384]{1,0:T(8,128)(2,1)S(1)}, u32[]{:S(2)}, u32[]{:S(2)}) collective-permute-start(bf16[192,384]{1,0:T(8,128)(2,1)S(1)} %get-tuple-element.301.refs_1_), channel_id=1, source_target_pairs={{0,16},{4,20},{8,24},{12,28},{16,0},{20,4},{24,8},{28,12},{1,17},{... | collective-permute-start | bytes 442376 | tf_op jit(solution)/shard_map/ppermute | solution.py:24
  128.2 13.3 %collective-permute-start.34 = (f32[2,256,128]{2,1,0:T(8,128)S(1)}, f32[2,256,128]{2,1,0:T(8,128)S(1)}, u32[]{:S(2)}, u32[]{:S(2)}) collective-permute-start(f32[2,256,128]{2,1,0:T(8,128)S(1)} %get-tuple-element.311), channel_id=1, source_target_pairs={{0,2},{1,3},{2,0},{3,1},{4,6},{5,7},{6,4},{7,5},{8,10},{9,11},{10,... | collective-permute-start | bytes 786440 | tf_op jit(solution)/shard_map/ppermute | solution.py:24
  129.0 9.5 %collective-permute-start.30 = (bf16[384,384]{1,0:T(8,128)(2,1)S(1)}, bf16[384,384]{1,0:T(8,128)(2,1)S(1)}, u32[]{:S(2)}, u32[]{:S(2)}) collective-permute-start(bf16[384,384]{1,0:T(8,128)(2,1)S(1)} %get-tuple-element.297), channel_id=1, source_target_pairs={{0,4},{4,0},{8,12},{12,8},{16,20},{20,16},{24,28},{28,24},{1,5},{5... | collective-permute-start | bytes 884744 | tf_op jit(solution)/shard_map/ppermute | solution.py:24
  137.9 17.5 %collective-permute-start.37 = (bf16[384,384]{1,0:T(8,128)(2,1)S(1)}, bf16[384,384]{1,0:T(8,128)(2,1)S(1)}, u32[]{:S(2)}, u32[]{:S(2)}) collective-permute-start(bf16[384,384]{1,0:T(8,128)(2,1)S(1)} %get-tuple-element.329.refs_1_), channel_id=1, source_target_pairs={{0,8},{4,12},{8,0},{12,4},{16,24},{20,28},{24,16},{28,20},{1,9},{5... | collective-permute-start | bytes 884744 | tf_op jit(solution)/shard_map/ppermute | solution.py:24
  139.1 10.6 %collective-permute-start.33 = (bf16[192,384]{1,0:T(8,128)(2,1)S(1)}, bf16[192,384]{1,0:T(8,128)(2,1)S(1)}, u32[]{:S(2)}, u32[]{:S(2)}) collective-permute-start(bf16[192,384]{1,0:T(8,128)(2,1)S(1)} %get-tuple-element.309), channel_id=1, source_target_pairs={{0,8},{4,12},{8,0},{12,4},{16,24},{20,28},{24,16},{28,20},{1,9},{5... | collective-permute-start | bytes 442376 | tf_op jit(solution)/shard_map/ppermute | solution.py:24
  145.5 11.2 %collective-permute-start.36 = (bf16[4,16,512]{2,1,0:T(8,128)(2,1)S(1)}, bf16[4,16,512]{2,1,0:T(8,128)(2,1)S(1)}, u32[]{:S(2)}, u32[]{:S(2)}) collective-permute-start(bf16[4,16,512]{2,1,0:T(8,128)(2,1)S(1)} %get-tuple-element.326), channel_id=1, source_target_pairs={{4,0},{8,4},{12,8},{16,12},{20,16},{24,20},{28,24},{5,1},{9,5},{13... | collective-permute-start | bytes 196616 | tf_op jit(solution)/shard_map/ppermute | solution.py:24
  150.3 10.4 %collective-permute-start.35 = (bf16[96,384]{1,0:T(8,128)(2,1)S(1)}, bf16[96,384]{1,0:T(8,128)(2,1)S(1)}, u32[]{:S(2)}, u32[]{:S(2)}) collective-permute-start(bf16[96,384]{1,0:T(8,128)(2,1)S(1)} %get-tuple-element.324), channel_id=1, source_target_pairs={{0,16},{4,20},{8,24},{12,28},{16,0},{20,4},{24,8},{28,12},{1,17},{... | collective-permute-start | bytes 221192 | tf_op jit(solution)/shard_map/ppermute | solution.py:24
  156.1 16.5 %collective-permute-start.45 = (bf16[768,384]{1,0:T(8,128)(2,1)S(1)}, bf16[768,384]{1,0:T(8,128)(2,1)S(1)}, u32[]{:S(2)}, u32[]{:S(2)}) collective-permute-start(bf16[768,384]{1,0:T(8,128)(2,1)S(1)} %get-tuple-element.356.refs_1_), channel_id=1, source_target_pairs={{0,4},{4,0},{8,12},{12,8},{16,20},{20,16},{24,28},{28,24},{1,5},{5... | collective-permute-start | bytes 1769480 | tf_op jit(solution)/shard_map/ppermute | solution.py:24
  169.1 7.8 %collective-permute-start.44 = (bf16[192,384]{1,0:T(8,128)(2,1)S(1)}, bf16[192,384]{1,0:T(8,128)(2,1)S(1)}, u32[]{:S(2)}, u32[]{:S(2)}) collective-permute-start(bf16[192,384]{1,0:T(8,128)(2,1)S(1)} %get-tuple-element.355.refs_1_), channel_id=1, source_target_pairs={{0,8},{4,12},{8,0},{12,4},{16,24},{20,28},{24,16},{28,20},{1,9},{5... | collective-permute-start | bytes 442376 | tf_op jit(solution)/shard_map/ppermute | solution.py:24
  169.3 9.4 %collective-permute-start.42 = (bf16[192,384]{1,0:T(8,128)(2,1)S(1)}, bf16[192,384]{1,0:T(8,128)(2,1)S(1)}, u32[]{:S(2)}, u32[]{:S(2)}) collective-permute-start(bf16[192,384]{1,0:T(8,128)(2,1)S(1)} %get-tuple-element.351.refs_0_), channel_id=1, source_target_pairs={{0,16},{4,20},{8,24},{12,28},{16,0},{20,4},{24,8},{28,12},{1,17},{... | collective-permute-start | bytes 442376 | tf_op jit(solution)/shard_map/ppermute | solution.py:24
  171.9 11.1 %collective-permute-start.41 = (bf16[4,208,256]{2,1,0:T(8,128)(2,1)S(1)}, bf16[4,208,256]{2,1,0:T(8,128)(2,1)S(1)}, u32[]{:S(2)}, u32[]{:S(2)}) collective-permute-start(bf16[4,208,256]{2,1,0:T(8,128)(2,1)S(1)} %get-tuple-element.345), channel_id=1, source_target_pairs={{0,2},{1,3},{2,0},{3,1},{4,6},{5,7},{6,4},{7,5},{8,10},{9,11},{10,... | collective-permute-start | bytes 1277960 | tf_op jit(solution)/shard_map/ppermute | solution.py:24
  179.5 9.4 %collective-permute-start.48 = (bf16[384,384]{1,0:T(8,128)(2,1)S(1)}, bf16[384,384]{1,0:T(8,128)(2,1)S(1)}, u32[]{:S(2)}, u32[]{:S(2)}) collective-permute-start(bf16[384,384]{1,0:T(8,128)(2,1)S(1)} %get-tuple-element.367.refs_1_), channel_id=1, source_target_pairs={{0,4},{4,0},{8,12},{12,8},{16,20},{20,16},{24,28},{28,24},{1,5},{5... | collective-permute-start | bytes 884744 | tf_op jit(solution)/shard_map/ppermute | solution.py:24
  (70 other events, 415.0 us)
